TPU v7x, 32 devices: a whole 2x2x4 slice. The times are simulated.
32 devices in a mesh: sector: 8 (over z, y), dof: 4 (over x, core).
Axes of the slice: x: 2, y: 2, z: 4, core: 2. Of those that a mesh axis runs over, the one named last changes fastest.
Arguments:
- load_history: bfloat16 [8, 64, 6144], P('sector', None, 'dof'), may hold values from -6 to 6
- sector_basis: bfloat16 [6144, 1536], P('dof'), may hold values from -0.078125 to 0.078125
- harmonic_modes: bfloat16 [8, 1536, 256], P('sector'), may hold values from -0.15625 to 0.15625
- stress_basis: bfloat16 [1536, 6144], P(None, 'dof'), may hold values from -0.375 to 0.375
- mode_decay: float32 [8, 256], P('sector'), may hold values from 0.01 to 0.3
- mode_phase: float32 [8, 256], P('sector'), may hold values from 0.05 to 1.5
- mode_count: int32 [8], P('sector'), may hold values from 64 to 256, as said below
- slot_harmonic: int32 [8], replicated, may hold values from 0 to 7, each once
Outputs:
- stress_field: bfloat16 [8, 64, 6144], P('sector', None, 'dof')
Inputs may be any that keep to these rules, and one draw needn't show every extreme that they name: Slot modes from mode_count on are left out; some slot has 256 live modes and some 256 // 4. `slot_harmonic`: every harmonic component is held by exactly one slot.
All inputs are finite; a program needn't handle non-finite values.
Results may differ from a plain program's by a relative error of at most 0.025.
Values may be sent and summed in bfloat16 or wider, within the bound.
A program may use at most 64 MiB of HBM per device.

v0:
```python
import math

import jax
import jax.numpy as jnp
from jax import lax
from jax.sharding import PartitionSpec as P


def transform_table(slot_harmonic):
    count_all = slot_harmonic.shape[0]
    half_count = count_all // 2
    sine_rows = slot_harmonic > half_count
    harmonic_order = jnp.where(sine_rows, slot_harmonic - half_count, slot_harmonic)
    sector_index = jnp.arange(count_all, dtype=jnp.int32)
    residue = harmonic_order[:, None] * sector_index[None, :] % count_all
    phase_angle = residue.astype(jnp.float32) * jnp.float32(2.0 * math.pi / count_all)
    wave_table = jnp.where(sine_rows[:, None], jnp.sin(phase_angle), jnp.cos(phase_angle))
    single = (slot_harmonic == 0) | (slot_harmonic == half_count)
    weight = jnp.where(single, jnp.float32(1.0 / count_all), jnp.float32(2.0 / count_all))
    return jnp.sqrt(weight)[:, None] * wave_table


def filter_kernel(decay_rates, phase_steps, steps_count):
    time_index = jnp.arange(steps_count, dtype=jnp.int32)
    offset = time_index[:, None] - time_index[None, :]
    causal = offset >= 0
    lag_value = jnp.maximum(offset, 0).astype(jnp.float32)
    gain_factor = jnp.sqrt(1.0 - jnp.exp(-2.0 * decay_rates))
    shape_table = (
        gain_factor[..., None, None]
        * jnp.exp(-decay_rates[..., None, None] * lag_value)
        * jnp.cos(phase_steps[..., None, None] * lag_value)
    )
    return jnp.where(causal, shape_table, jnp.float32(0.0))


def local(
    load_history,
    sector_basis,
    harmonic_modes,
    stress_basis,
    mode_decay,
    mode_phase,
    mode_count,
    slot_harmonic,
):
    highest = lax.Precision.HIGHEST
    table = transform_table(slot_harmonic)
    steps_count = load_history.shape[1]
    modes_slot = harmonic_modes[0]
    partial_value = jnp.dot(load_history[0], sector_basis, preferred_element_type=jnp.float32)
    live = (jnp.arange(modes_slot.shape[1], dtype=jnp.int32) < mode_count[0]).astype(jnp.float32)
    kernel = filter_kernel(mode_decay[0], mode_phase[0], steps_count)
    reduced = lax.psum(partial_value.astype(jnp.bfloat16), "dof")
    mixed = jnp.einsum(
        "ks,stc->ktc",
        table,
        lax.all_to_all(reduced[None], "sector", split_axis=1, concat_axis=0, tiled=True).astype(
            jnp.float32
        ),
        precision=highest,
    )
    spectrum = lax.all_to_all(
        mixed.astype(jnp.bfloat16), "sector", split_axis=0, concat_axis=1, tiled=True
    )[0]
    modal = jnp.dot(spectrum, modes_slot, preferred_element_type=jnp.float32) * live[None, :]
    response = jnp.einsum("mtu,um->tm", kernel, modal, precision=highest)
    project_response = response.astype(jnp.bfloat16)
    product = lax.dot_general(
        project_response, modes_slot, (((1,), (1,)), ((), ())), preferred_element_type=jnp.float32
    )
    returned = product.astype(jnp.bfloat16)
    mixed = jnp.einsum(
        "ks,ktc->stc",
        table,
        lax.all_to_all(returned[None], "sector", split_axis=1, concat_axis=0, tiled=True).astype(
            jnp.float32
        ),
        precision=highest,
    )
    back = lax.all_to_all(
        mixed.astype(jnp.bfloat16), "sector", split_axis=0, concat_axis=1, tiled=True
    )[0]
    stress_field = jnp.dot(back, stress_basis, preferred_element_type=jnp.float32).astype(
        jnp.bfloat16
    )
    return stress_field[None]


def solution(mesh):
    return jax.shard_map(
        local,
        mesh=mesh,
        in_specs=(
            P("sector", None, "dof"),
            P("dof", None),
            P("sector", None, None),
            P(None, "dof"),
            P("sector", None),
            P("sector", None),
            P("sector"),
            P(),
        ),
        out_specs=P("sector", None, "dof"),
        check_vma=False,
    )
```

profile of v0, /device:TPU:0, one launch (start us, length us, event | category | flops | bytes accessed | tf_op | source)
XLA Modules:
  0.0 126.2 jit_solution(13284752382754742278)
XLA Ops:
  6.6 4.1 %fusion.1 = bf16[1,64,1536]{2,1,0:T(8,128)(2,1)} fusion(bf16[1536,1536]{1,0:T(8,128)(2,1)} %param.9, bf16[1,64,1536]{2,1,0:T(8,128)(2,1)} %param.8), kind=kOutput, calls=%fused_computation.7 | convolution fusion | flops 302088192 | bytes 5111808 | tf_op jit(solution)/shard_map/dot_general | solution.py:51
  10.7 34.5 %all-reduce.2.cloned.1.call-done = bf16[1,64,1536]{2,1,0:T(8,128)(2,1)} async-done(((bf16[1,64,1536]{2,1,0:T(8,128)(2,1)}), bf16[1,64,1536]{2,1,0:T(8,128)(2,1)}) %all-reduce.2.cloned.1.call-update) | async-done | bytes 196624 | tf_op jit(solution)/shard_map/psum | solution.py:54
  45.2 1.2 copy.59
  46.5 0.5 broadcast.67
  47.0 1.7 %reduce.2 = bf16[64,1536]{1,0:T(8,128)(2,1)S(1)} reduce(bf16[64,1,1536]{2,1,0:T(2,128)(2,1)S(1)} %bitcast.54, bf16[]{:T(256)} %broadcast.67), dimensions={1}, to_apply=%bitcast.50.reduce_sub_computation | reduce | bytes 393218
  48.7 0.8 reshape.63
  49.4 5.5 %all-to-all-start = ((bf16[8,2,6144]{2,1,0:T(2,128)(2,1)}), bf16[8,2,6144]{2,1,0:T(2,128)(2,1)S(1)}, u32[]{:S(2)}, u32[]{:S(2)}) async-start(bf16[8,2,6144]{2,1,0:T(2,128)(2,1)} %reshape.63), calls=%async_computation | async-start | bytes 393216 | tf_op jit(solution)/shard_map/all_to_all | solution.py:58
  55.7 7.1 %all-to-all-done = bf16[8,2,6144]{2,1,0:T(2,128)(2,1)S(1)} async-done(((bf16[8,2,6144]{2,1,0:T(2,128)(2,1)}), bf16[8,2,6144]{2,1,0:T(2,128)(2,1)S(1)}, u32[]{:S(2)}, u32[]{:S(2)}) %all-to-all-start) | async-done | bytes 196640 | tf_op jit(solution)/shard_map/all_to_all | solution.py:58
  62.7 0.2 reshape.64
  63.0 0.4 convolution_convert_fusion.3
  63.4 0.7 copy.32
  64.1 3.4 %all-to-all-start.1 = ((bf16[8,8,1536]{2,1,0:T(8,128)(2,1)}), bf16[8,8,1536]{2,1,0:T(8,128)(2,1)S(1)}, u32[]{:S(2)}, u32[]{:S(2)}) async-start(bf16[8,8,1536]{2,1,0:T(8,128)(2,1)} %copy.32), calls=%async_computation.1 | async-start | bytes 393216 | tf_op jit(solution)/shard_map/all_to_all | solution.py:63
  67.6 7.7 %all-to-all-done.1 = bf16[8,8,1536]{2,1,0:T(8,128)(2,1)S(1)} async-done(((bf16[8,8,1536]{2,1,0:T(8,128)(2,1)}), bf16[8,8,1536]{2,1,0:T(8,128)(2,1)S(1)}, u32[]{:S(2)}, u32[]{:S(2)}) %all-to-all-start.1) | async-done | bytes 196640 | tf_op jit(solution)/shard_map/all_to_all | solution.py:63
  75.3 0.3 fusion.3
  75.5 16.2 %multiply_reduce_fusion = bf16[256,64]{0,1:T(8,128)(2,1)S(1)} fusion(f32[256,64]{0,1:T(8,128)S(1)} %fusion.3, f32[256]{0:T(256)S(1)} %bitcast.60, f32[64,64]{1,0:T(8,128)S(1)} %maximum_convert_fusion, f32[256]{0:T(256)S(1)} %bitcast.59, f32[256]{0:T(256)S(1)} %bitcast.58, pred[64,64]{1,0:T(8,128)(4,1)S(1)} %fusion.12), kind=kLoop, calls=%fused_computation | loop fusion | flops 7323648 | bytes 121856
  91.8 0.1 copy.43
  91.9 0.4 fusion
  92.3 0.3 copy.58
  92.6 1.7 %reduce.3 = bf16[64,1536]{1,0:T(8,128)(2,1)S(1)} reduce(bf16[64,1,1536]{2,1,0:T(2,128)(2,1)S(1)} %bitcast.55, bf16[]{:T(256)} %broadcast.67), dimensions={1}, to_apply=%bitcast.49.reduce_sub_computation | reduce | bytes 393218
  94.4 10.2 %all_to_all.42 = bf16[8,2,6144]{2,1,0:T(2,128)(2,1)S(1)} all-to-all(bf16[8,2,6144]{2,1,0:T(2,128)(2,1)S(1)} %reshape.65), channel_id=1, replica_groups=mesh['sector'=8,'dof'=4] {'sector'}, dimensions={0} | all-to-all | bytes 393216 | tf_op jit(solution)/shard_map/all_to_all | solution.py:76
  104.6 0.2 reshape.66
  104.8 0.4 convolution_convert_fusion.1
  105.2 10.2 %all_to_all.43 = bf16[8,8,1536]{2,1,0:T(8,128)(2,1)S(1)} all-to-all(bf16[8,8,1536]{2,1,0:T(8,128)(2,1)S(1)} %copy.35), channel_id=1, replica_groups=mesh['sector'=8,'dof'=4] {'sector'}, dimensions={0} | all-to-all | bytes 393216 | tf_op jit(solution)/shard_map/all_to_all | solution.py:81
  115.4 3.9 %fusion.2 = bf16[1,64,1536]{2,1,0:T(8,128)(2,1)} fusion(bf16[1536,1536]{1,0:T(8,128)(2,1)} %param.11, bf16[8,8,1536]{2,1,0:T(8,128)(2,1)S(1)} %all_to_all.43), kind=kOutput, calls=%fused_computation.8 | convolution fusion | flops 302088192 | bytes 5111808 | tf_op jit(solution)/shard_map/dot_general | solution.py:84
  (21 shorter events, 0.3 us)
Async XLA Ops:
  6.5 68.7 %copy-start = (bf16[1,1536,256]{2,1,0:T(8,128)(2,1)S(1)}, bf16[1,1536,256]{2,1,0:T(8,128)(2,1)}, u32[]{:S(2)}) copy-start(bf16[1,1536,256]{2,1,0:T(8,128)(2,1)} %param.10) | copy-start | bytes 2359300
  6.5 4.2 %copy-start.3 = (s32[8]{0:T(128)S(1)}, s32[8]{0:T(128)}, u32[]{:S(2)}) copy-start(s32[8]{0:T(128)} %param.15) | copy-start | bytes 100
  6.5 61.0 %copy-start.1 = (f32[1,256]{1,0:T(1,128)S(1)}, f32[1,256]{1,0:T(1,128)}, u32[]{:S(2)}) copy-start(f32[1,256]{1,0:T(1,128)} %param.12) | copy-start | bytes 3076
  6.5 69.0 %copy-start.2 = (f32[1,256]{1,0:T(1,128)S(1)}, f32[1,256]{1,0:T(1,128)}, u32[]{:S(2)}) copy-start(f32[1,256]{1,0:T(1,128)} %param.13) | copy-start | bytes 3076
  6.5 38.7 %all-reduce.2.cloned.1.call-start = ((), (), s32[]{:S(2)}) async-start(), calls=%async_computation.4 | async-start | bytes 393216 | tf_op jit(solution)/shard_map/psum | solution.py:54
  49.4 13.3 %all-to-all-start = ((bf16[8,2,6144]{2,1,0:T(2,128)(2,1)}), bf16[8,2,6144]{2,1,0:T(2,128)(2,1)S(1)}, u32[]{:S(2)}, u32[]{:S(2)}) async-start(bf16[8,2,6144]{2,1,0:T(2,128)(2,1)} %reshape.63), calls=%async_computation | async-start | bytes 393216 | tf_op jit(solution)/shard_map/all_to_all | solution.py:58
  64.1 11.1 %all-to-all-start.1 = ((bf16[8,8,1536]{2,1,0:T(8,128)(2,1)}), bf16[8,8,1536]{2,1,0:T(8,128)(2,1)S(1)}, u32[]{:S(2)}, u32[]{:S(2)}) async-start(bf16[8,8,1536]{2,1,0:T(8,128)(2,1)} %copy.32), calls=%async_computation.1 | async-start | bytes 393216 | tf_op jit(solution)/shard_map/all_to_all | solution.py:63
Sparse Core Ops, SparseCore 0:
  10.8 34.3 all-reduce.1
where the time goes:
time: 127 us; the launch traced here: 126 us
  waiting for transfers between devices  49.3 us (39%)
  blocking collectives  20.4 us (16%)
  other arithmetic  19.7 us (16%)
  between operations  14.2 us (11%)
  matrix products  9.47 us (7%)
  starting transfers between devices  8.94 us (7%)
  local copies, waits for them, and re-layouts  4.21 us (3%)
    psum x1, waiting for transfers between devices, local(): reduced = lax.psum(partial_value.astype(jnp.bfloat16), 'dof')  34.5 us
    unnamed x3, other arithmetic  19.6 us
    all_to_all x1, blocking collectives, local(): lax.all_to_all(mixed.astype(jnp.bfloat16), 'sector', split_axis=0, concat...  10.2 us
    all_to_all x1, blocking collectives, local(): lax.all_to_all(returned[None], 'sector', split_axis=1, concat_axis=0, til...  10.2 us
    all_to_all x1, waiting for transfers between devices, local(): lax.all_to_all(mixed.astype(jnp.bfloat16), 'sector', split_axis=0, concat...  7.66 us
    all_to_all x1, waiting for transfers between devices, local(): lax.all_to_all(reduced[None], 'sector', split_axis=1, concat_axis=0, tile...  7.09 us
    all_to_all x1, starting transfers between devices, local(): lax.all_to_all(reduced[None], 'sector', split_axis=1, concat_axis=0, tile...  5.52 us
    dot_general x1, matrix products, local(): jnp.dot(load_history[0], sector_basis, preferred_element_type=jnp.float32)  4.11 us
  transfers between devices with their start and end apart: 3, of which 3 were waited for; matrix products, arithmetic and copies ran while one was open for 0% of the time, Pallas kernels for 0%

commit v1 on v0

v1 whole, which is shorter than its diff:
```python
import functools
import math

import jax
import jax.numpy as jnp
from jax import lax
from jax.experimental import pallas as pl
from jax.experimental.pallas import tpu as pltpu
from jax.sharding import PartitionSpec as P

MESH = pl.DeviceIdType.MESH
ROWS = 16
HALVES = 2


def each(count, body):
    if count <= 32:
        for index in range(count):
            body(index)
    else:

        @pl.loop(0, count)
        def _(index):
            body(index)


def kernel(
    sectors,
    dofs,
    load_hbm,
    basis_hbm,
    modes_hbm,
    stress_hbm,
    decay_ref,
    phase_ref,
    count_ref,
    slot_ref,
    out_ref,
    load_v,
    basis_v,
    modes_v,
    stress_v,
    part_send,
    part_recv,
    spec_send,
    spec_recv,
    ret_send,
    ret_recv,
    back_send,
    back_recv,
    fwd_table,
    bwd_table,
    lag_table,
    padded,
    local_sem,
    basis_sem,
    send_sem,
    part_sem,
    spec_sem,
    ret_sem,
    back_sem,
):
    steps, reduced = load_v.shape
    width = reduced // dofs
    half = reduced // HALVES
    groups = steps // ROWS
    per_half = dofs // HALVES
    mixers = groups * dofs
    devices = sectors * dofs
    stride = devices // mixers
    f32, bf16 = jnp.float32, jnp.bfloat16

    own_sector = lax.axis_index("sector")
    own_dof = lax.axis_index("dof")
    me = own_sector * dofs + own_dof
    is_mixer = lax.rem(me, stride) == 0
    own_piece = me // stride
    own_group = own_piece // dofs
    own_rest = lax.rem(own_piece, dofs)
    own_part = lax.rem(own_rest, HALVES) * per_half + own_rest // HALVES

    def device(index):
        return (index // dofs, lax.rem(index, dofs))

    def mixer_of(group, part):
        return (group * dofs + lax.rem(part, per_half) * HALVES + part // per_half) * stride

    load_copy = pltpu.make_async_copy(load_hbm.at[0], load_v, local_sem.at[0])
    load_copy.start()
    basis_copies = []
    for turn in range(HALVES):
        which = lax.rem(own_sector + own_dof + turn, HALVES)
        columns = pl.ds(pl.multiple_of(which * half, 128), half)
        copy = pltpu.make_async_copy(
            basis_hbm.at[:, columns], basis_v.at[turn], basis_sem.at[turn]
        )
        copy.start()
        basis_copies.append(copy)
    modes_copy = pltpu.make_async_copy(modes_hbm.at[0], modes_v, local_sem.at[1])
    modes_copy.start()
    stress_copy = pltpu.make_async_copy(stress_hbm, stress_v, local_sem.at[2])
    stress_copy.start()

    barrier = pltpu.get_barrier_semaphore()

    def greet_mixer(index):
        target = index * stride

        @pl.when(target != me)
        def _():
            pl.semaphore_signal(barrier, inc=1, device_id=device(target), device_id_type=MESH)

    each(mixers, greet_mixer)

    @pl.when(is_mixer)
    def _():
        def greet_other(index):
            target = index // (stride - 1) * stride + 1 + index % (stride - 1)
            pl.semaphore_signal(barrier, inc=1, device_id=device(target), device_id_type=MESH)

        each(devices - mixers, greet_other)

    def send_to(src, dst, sem, out_sem, target):
        @pl.when(target != me)
        def _():
            pltpu.make_async_remote_copy(
                src_ref=src,
                dst_ref=dst,
                send_sem=out_sem,
                recv_sem=sem,
                device_id=device(target),
                device_id_type=MESH,
            ).start()

        @pl.when(target == me)
        def _():
            pltpu.make_async_copy(src, dst, sem).start()

    load_copy.wait()
    for turn in range(HALVES):
        which = lax.rem(own_sector + own_dof + turn, HALVES)
        basis_copies[turn].wait()
        product = jnp.dot(load_v[...], basis_v[turn], preferred_element_type=f32).astype(bf16)
        for inner in range(per_half):
            part_send[turn, inner] = product[:, inner * width : (inner + 1) * width].reshape(
                groups, ROWS, width
            )
        if turn == 0:

            @pl.when(is_mixer)
            def _():
                pl.semaphore_wait(barrier, devices - 1)

            @pl.when(jnp.logical_not(is_mixer))
            def _():
                pl.semaphore_wait(barrier, mixers)

        for inner in range(per_half):
            part = which * per_half + inner
            for group in range(groups):
                send_to(
                    part_send.at[turn, inner, group],
                    part_recv.at[own_sector, own_dof],
                    part_sem,
                    send_sem.at[0],
                    mixer_of(group, part),
                )

    decay = decay_ref[...]
    lag = lax.broadcasted_iota(jnp.int32, lag_table.shape, 0).astype(f32)
    gain = jnp.sqrt(1.0 - jnp.exp(-2.0 * decay))
    lag_table[...] = gain * jnp.exp(-decay * lag) * jnp.cos(phase_ref[...] * lag)
    padded[pl.ds(0, steps), :] = jnp.zeros((steps, padded.shape[1]), f32)

    @pl.when(is_mixer)
    def _():
        wide = sectors * ROWS
        row = lax.broadcasted_iota(jnp.int32, (sectors, wide), 0)
        sector = (lax.broadcasted_iota(jnp.int32, (sectors, wide), 1) // ROWS).astype(f32)
        harmonic = jnp.zeros((sectors, wide), f32)
        for slot in range(sectors):
            harmonic = jnp.where(row == slot, slot_ref[slot].astype(f32), harmonic)
        middle = float(sectors // 2)
        sine = harmonic > middle
        order = jnp.where(sine, harmonic - middle, harmonic)
        turns = order * sector
        residue = turns - float(sectors) * jnp.floor(turns * (1.0 / sectors))
        angle = residue * jnp.float32(2.0 * math.pi / sectors)
        wave = jnp.cos(angle - jnp.where(sine, jnp.float32(0.5 * math.pi), jnp.float32(0.0)))
        single = (harmonic == 0.0) | (harmonic == middle)
        weight = jnp.where(single, jnp.float32(math.sqrt(1.0 / sectors)), jnp.float32(math.sqrt(2.0 / sectors)))
        small = weight * wave
        table = jnp.broadcast_to(small[:, None, :], (sectors, ROWS, wide)).reshape(wide, wide)
        left = lax.broadcasted_iota(jnp.int32, (wide, wide), 0) % ROWS
        right = lax.broadcasted_iota(jnp.int32, (wide, wide), 1) % ROWS
        table = jnp.where(left == right, table, 0.0)
        for where_to, values in ((fwd_table, table), (bwd_table, table.T)):
            high = values.astype(bf16)
            where_to[0] = high
            where_to[1] = (values - high.astype(f32)).astype(bf16)

    def mix(table_ref, values):
        return (
            jnp.dot(table_ref[0], values, preferred_element_type=f32)
            + jnp.dot(table_ref[1], values, preferred_element_type=f32)
        ).astype(bf16)

    own_half = own_part // per_half
    own_columns = pl.ds(pl.multiple_of(lax.rem(own_part, per_half) * width, 128), width)

    def spread(source, sink, sem, out_sem):
        dst = sink.at[own_half, own_group, :, own_columns]

        def send(index):
            target = lax.rem(me + index + 1, devices)
            pltpu.make_async_remote_copy(
                src_ref=source.at[target // dofs],
                dst_ref=dst,
                send_sem=out_sem,
                recv_sem=sem.at[own_half],
                device_id=device(target),
                device_id_type=MESH,
            ).start()

        each(devices - 1, send)
        pltpu.make_async_copy(source.at[own_sector], dst, sem.at[own_half]).start()

    @pl.when(is_mixer)
    def _():
        pltpu.make_async_copy(part_recv, part_recv, part_sem).wait()
        total = part_recv[:, 0].astype(f32)
        for dof in range(1, dofs):
            total = total + part_recv[:, dof].astype(f32)
        values = total.reshape(sectors * ROWS, width).astype(bf16)
        spec_send[...] = mix(fwd_table, values).reshape(sectors, ROWS, width)
        spread(spec_send, spec_recv, spec_sem, send_sem.at[1])

    modes_copy.wait()
    modal = jnp.zeros((steps, modes_v.shape[1]), f32)
    for which in range(HALVES):
        pltpu.make_async_copy(
            spec_recv.at[which], spec_recv.at[which], spec_sem.at[which]
        ).wait()
        modal = modal + jnp.dot(
            spec_recv[which].reshape(steps, half),
            modes_v[pl.ds(which * half, half), :],
            preferred_element_type=f32,
        )
    mode = lax.broadcasted_iota(jnp.int32, modal.shape, 1)
    padded[pl.ds(steps, steps), :] = jnp.where(mode < count_ref[0], modal, 0.0)
    cut = steps // 2
    upper = jnp.zeros((cut, modal.shape[1]), f32)
    lower = jnp.zeros((cut, modal.shape[1]), f32)
    for n in range(steps):
        scale = lag_table[pl.ds(n, 1), :]
        if n < cut:
            upper = upper + scale * padded[pl.ds(steps - n, cut), :]
        lower = lower + scale * padded[pl.ds(steps + cut - n, cut), :]
    response = jnp.concatenate([upper, lower], axis=0).astype(bf16)
    own_rows = modes_v[pl.ds(pl.multiple_of(own_dof * width, 128), width), :]
    returned = lax.dot_general(
        response, own_rows, (((1,), (1,)), ((), ())), preferred_element_type=f32
    )
    ret_send[...] = returned.astype(bf16).reshape(groups, ROWS, width)
    for group in range(groups):
        send_to(
            ret_send.at[group],
            ret_recv.at[own_sector],
            ret_sem,
            send_sem.at[2],
            mixer_of(group, own_dof),
        )

    @pl.when(is_mixer)
    def _():
        pltpu.make_async_copy(ret_recv, ret_recv, ret_sem).wait()
        values = ret_recv[...].reshape(sectors * ROWS, width)
        back_send[...] = mix(bwd_table, values).reshape(sectors, ROWS, width)
        spread(back_send, back_recv, back_sem, send_sem.at[3])

    stress_copy.wait()
    field = jnp.zeros((steps, out_ref.shape[2]), f32)
    for which in range(HALVES):
        pltpu.make_async_copy(
            back_recv.at[which], back_recv.at[which], back_sem.at[which]
        ).wait()
        field = field + jnp.dot(
            back_recv[which].reshape(steps, half),
            stress_v[pl.ds(which * half, half), :],
            preferred_element_type=f32,
        )
    out_ref[0] = field.astype(bf16)

    def sent(ref, sem):
        pltpu.make_async_copy(ref, ref, sem).wait()

    @pl.when(is_mixer)
    def _():
        for index in range(dofs):
            ref = part_send.at[index // per_half, index % per_half]
            sent(ref.at[pl.ds(0, groups - (index == 0))], send_sem.at[0])
        for sem in (send_sem.at[1], send_sem.at[3]):
            sent(part_recv.at[pl.ds(0, sectors - 1)], sem)
            sent(part_recv.at[0, pl.ds(0, dofs - 1)], sem)

    @pl.when(jnp.logical_not(is_mixer))
    def _():
        sent(part_send, send_sem.at[0])

    own_return = is_mixer & (own_part == own_dof)

    @pl.when(own_return)
    def _():
        sent(ret_send.at[pl.ds(0, groups - 1)], send_sem.at[2])

    @pl.when(jnp.logical_not(own_return))
    def _():
        sent(ret_send, send_sem.at[2])


def local(
    sectors,
    dofs,
    load_history,
    sector_basis,
    harmonic_modes,
    stress_basis,
    mode_decay,
    mode_phase,
    mode_count,
    slot_harmonic,
):
    _, steps, rows = load_history.shape
    reduced = sector_basis.shape[1]
    modes = harmonic_modes.shape[2]
    stress = stress_basis.shape[1]
    width = reduced // dofs
    groups = steps // ROWS
    half = reduced // HALVES
    wide = sectors * ROWS
    bf16, f32 = jnp.bfloat16, jnp.float32
    flops = 2 * steps * reduced * (rows + stress + 2 * modes)
    return pl.pallas_call(
        functools.partial(kernel, sectors, dofs),
        out_shape=jax.ShapeDtypeStruct((1, steps, stress), bf16),
        in_specs=[pl.BlockSpec(memory_space=pl.ANY)] * 4
        + [pl.BlockSpec(memory_space=pltpu.VMEM)] * 2
        + [pl.BlockSpec(memory_space=pltpu.SMEM)] * 2,
        out_specs=pl.BlockSpec(memory_space=pltpu.VMEM),
        scratch_shapes=[
            pltpu.VMEM((steps, rows), bf16),
            pltpu.VMEM((HALVES, rows, half), bf16),
            pltpu.VMEM((reduced, modes), bf16),
            pltpu.VMEM((reduced, stress), bf16),
            pltpu.VMEM((HALVES, dofs // HALVES, groups, ROWS, width), bf16),
            pltpu.VMEM((sectors, dofs, ROWS, width), bf16),
            pltpu.VMEM((sectors, ROWS, width), bf16),
            pltpu.VMEM((HALVES, groups, ROWS, half), bf16),
            pltpu.VMEM((groups, ROWS, width), bf16),
            pltpu.VMEM((sectors, ROWS, width), bf16),
            pltpu.VMEM((sectors, ROWS, width), bf16),
            pltpu.VMEM((HALVES, groups, ROWS, half), bf16),
            pltpu.VMEM((2, wide, wide), bf16),
            pltpu.VMEM((2, wide, wide), bf16),
            pltpu.VMEM((steps, modes), f32),
            pltpu.VMEM((2 * steps, modes), f32),
            pltpu.SemaphoreType.DMA((3,)),
            pltpu.SemaphoreType.DMA((HALVES,)),
            pltpu.SemaphoreType.DMA((4,)),
            pltpu.SemaphoreType.DMA,
            pltpu.SemaphoreType.DMA((HALVES,)),
            pltpu.SemaphoreType.DMA,
            pltpu.SemaphoreType.DMA((HALVES,)),
        ],
        compiler_params=pltpu.CompilerParams(
            collective_id=0, has_side_effects=True, vmem_limit_bytes=48 * 1024 * 1024
        ),
        cost_estimate=pl.CostEstimate(
            flops=flops, bytes_accessed=2 * reduced * (rows + stress), transcendentals=0
        ),
    )(
        load_history,
        sector_basis,
        harmonic_modes,
        stress_basis,
        mode_decay,
        mode_phase,
        mode_count,
        slot_harmonic,
    )


def solution(mesh):
    return jax.shard_map(
        functools.partial(local, mesh.shape["sector"], mesh.shape["dof"]),
        mesh=mesh,
        in_specs=(
            P("sector", None, "dof"),
            P("dof", None),
            P("sector", None, None),
            P(None, "dof"),
            P("sector", None),
            P("sector", None),
            P("sector"),
            P(),
        ),
        out_specs=P("sector", None, "dof"),
        check_vma=False,
    )
```

time: 127 us -> 40.5 us (0.32)
  the two profiles are of different devices: /device:TPU:0 before, /device:TPU:1 now
where the time goes in v1:
time: 40.5 us; the launch traced here: 40 us
  Pallas kernels  32.2 us (80%)
  local copies, waits for them, and re-layouts  7.08 us (17%)
  between operations  0.67 us (2%)
    pallas_call x1, Pallas kernels, local(): pl.pallas_call(functools.partial(kernel, sectors, dofs), out_shape=jax.Sh...  32.2 us
    unnamed x13, local copies, waits for them, and re-layouts  7.08 us

profile of v1, /device:TPU:1, one launch (start us, length us, event | category | flops | bytes accessed | tf_op | source)
XLA Modules:
  0.0 40.0 jit_solution(16920860722898125385)
XLA Ops:
  0.7 0.0 copy-start
  0.7 2.3 %copy-done = bf16[1536,1536]{1,0:T(8,128)(2,1)S(1)} copy-done((bf16[1536,1536]{1,0:T(8,128)(2,1)S(1)}, bf16[1536,1536]{1,0:T(8,128)(2,1)}, u32[]{:S(2)}) %copy-start) | copy-done | bytes 4718616
  3.0 0.0 copy-start.1
  3.0 1.1 %copy-done.1 = bf16[1,1536,256]{2,1,0:T(8,128)(2,1)S(1)} copy-done((bf16[1,1536,256]{2,1,0:T(8,128)(2,1)S(1)}, bf16[1,1536,256]{2,1,0:T(8,128)(2,1)}, u32[]{:S(2)}) %copy-start.1) | copy-done | bytes 786456
  4.1 0.0 copy-start.2
  4.1 0.9 %copy-done.2 = bf16[1,64,1536]{2,1,0:T(8,128)(2,1)S(1)} copy-done((bf16[1,64,1536]{2,1,0:T(8,128)(2,1)S(1)}, bf16[1,64,1536]{2,1,0:T(8,128)(2,1)}, u32[]{:S(2)}) %copy-start.2) | copy-done | bytes 196632
  5.1 0.0 copy-start.3
  5.1 0.7 %copy-done.3 = f32[1,256]{1,0:T(1,128)S(1)} copy-done((f32[1,256]{1,0:T(1,128)S(1)}, f32[1,256]{1,0:T(1,128)}, u32[]{:S(2)}) %copy-start.3) | copy-done | bytes 1048
  5.7 0.0 copy-start.4
  5.7 0.7 %copy-done.4 = f32[1,256]{1,0:T(1,128)S(1)} copy-done((f32[1,256]{1,0:T(1,128)S(1)}, f32[1,256]{1,0:T(1,128)}, u32[]{:S(2)}) %copy-start.4) | copy-done | bytes 1048
  6.4 0.0 copy-start.5
  6.4 0.7 %copy-done.5 = s32[8]{0:T(128)S(1)} copy-done((s32[8]{0:T(128)S(1)}, s32[8]{0:T(128)}, u32[]{:S(2)}) %copy-start.5) | copy-done | bytes 56
  7.1 32.2 %shard_map.82 = bf16[1,64,1536]{2,1,0:T(8,128)(2,1)S(1)} custom-call(bf16[1,64,1536]{2,1,0:T(8,128)(2,1)S(1)} %copy-done.2, bf16[1536,1536]{1,0:T(8,128)(2,1)S(1)} %copy-done, bf16[1,1536,256]{2,1,0:T(8,128)(2,1)S(1)} %copy-done.1, bf16[1536,1536]{1,0:T(8,128)(2,1)} %stress_hbm.1, f32[1,256]{1,0:T(1,128)S(1)} %copy-done.3, f32[1,256]{1,0:T(1,128)S(1)} %copy-done.4, ...), custom_call_target="tpu_custom_call" | custom-call | flops 704643072 | bytes 9437184 | tf_op jit(solution)/shard_map/pallas_call | solution.py:343
  39.3 0.7 %copy.11 = bf16[1,64,1536]{2,1,0:T(8,128)(2,1)} copy(bf16[1,64,1536]{2,1,0:T(8,128)(2,1)S(1)} %shard_map.82) | data formatting | bytes 393216
Async XLA Ops:
  0.7 2.3 %copy-start = (bf16[1536,1536]{1,0:T(8,128)(2,1)S(1)}, bf16[1536,1536]{1,0:T(8,128)(2,1)}, u32[]{:S(2)}) copy-start(bf16[1536,1536]{1,0:T(8,128)(2,1)} %basis_hbm.1) | copy-start | bytes 14155780
  3.0 1.1 %copy-start.1 = (bf16[1,1536,256]{2,1,0:T(8,128)(2,1)S(1)}, bf16[1,1536,256]{2,1,0:T(8,128)(2,1)}, u32[]{:S(2)}) copy-start(bf16[1,1536,256]{2,1,0:T(8,128)(2,1)} %modes_hbm.1) | copy-start | bytes 2359300
  4.1 0.9 %copy-start.2 = (bf16[1,64,1536]{2,1,0:T(8,128)(2,1)S(1)}, bf16[1,64,1536]{2,1,0:T(8,128)(2,1)}, u32[]{:S(2)}) copy-start(bf16[1,64,1536]{2,1,0:T(8,128)(2,1)} %load_hbm.1) | copy-start | bytes 589828
  5.1 0.7 %copy-start.3 = (f32[1,256]{1,0:T(1,128)S(1)}, f32[1,256]{1,0:T(1,128)}, u32[]{:S(2)}) copy-start(f32[1,256]{1,0:T(1,128)} %decay_ref.1) | copy-start | bytes 3076
  5.7 0.7 %copy-start.4 = (f32[1,256]{1,0:T(1,128)S(1)}, f32[1,256]{1,0:T(1,128)}, u32[]{:S(2)}) copy-start(f32[1,256]{1,0:T(1,128)} %phase_ref.1) | copy-start | bytes 3076
  6.4 0.7 %copy-start.5 = (s32[8]{0:T(128)S(1)}, s32[8]{0:T(128)}, u32[]{:S(2)}) copy-start(s32[8]{0:T(128)} %slot_ref.1) | copy-start | bytes 100

commit v2 on v1

v2 whole, which is shorter than its diff:
```python
import functools
import math

import jax
import jax.numpy as jnp
from jax import lax
from jax.experimental import pallas as pl
from jax.experimental.pallas import tpu as pltpu
from jax.sharding import PartitionSpec as P

MESH = pl.DeviceIdType.MESH
ROWS = 16
HALVES = 2


def each(count, body):
    if count <= 32:
        for index in range(count):
            body(index)
    else:

        @pl.loop(0, count)
        def _(index):
            body(index)


def kernel(
    sectors,
    dofs,
    load_hbm,
    basis_hbm,
    modes_hbm,
    stress_hbm,
    decay_hbm,
    phase_hbm,
    count_hbm,
    slot_hbm,
    out_ref,
    load_v,
    basis_v,
    modes_v,
    stress_v,
    decay_v,
    phase_v,
    count_s,
    slot_s,
    pair_send,
    pair_recv,
    part_send,
    part_recv,
    spec_send,
    spec_recv,
    modal_send,
    modal_recv,
    ret_send,
    ret_recv,
    back_send,
    back_recv,
    back_other,
    fwd_table,
    bwd_table,
    lag_table,
    padded,
    local_sem,
    send_sem,
    recv_sem,
):
    steps, reduced = load_v.shape[0], stress_v.shape[0]
    width = reduced // dofs
    half = reduced // HALVES
    groups = steps // ROWS
    parts = dofs // HALVES
    spacing = sectors // (groups * HALVES)
    mixers = groups * parts
    peers = sectors * parts
    f32, bf16 = jnp.float32, jnp.bfloat16

    own_sector = lax.axis_index("sector")
    own_dof = lax.axis_index("dof")
    own_half = lax.rem(own_dof, HALVES)
    other_half = 1 - own_half
    own_pair = own_dof // HALVES
    me = own_sector * parts + own_pair
    own_place = own_sector // spacing
    own_group = own_place // HALVES
    is_mixer = (lax.rem(own_sector, spacing) == 0) & (lax.rem(own_place, HALVES) == own_half)
    sibling = (own_sector, own_pair * HALVES + other_half)

    def device(index):
        return (index // parts, lax.rem(index, parts) * HALVES + own_half)

    def mixer_of(group, part):
        return (group * HALVES + own_half) * spacing * parts + part

    def load(src, dst, index):
        copy = pltpu.make_async_copy(src, dst, local_sem.at[index])
        copy.start()
        return copy

    def columns_of(which):
        return pl.ds(pl.multiple_of(which * half, 128), half)

    load_copy = load(load_hbm.at[0], load_v, 0)
    other_copy = load(basis_hbm.at[:, columns_of(other_half)], basis_v.at[0], 1)
    own_copy = load(basis_hbm.at[:, columns_of(own_half)], basis_v.at[1], 2)
    slot_copy = load(slot_hbm, slot_s, 3)
    count_copy = load(count_hbm, count_s, 4)
    decay_copy = load(decay_hbm, decay_v, 5)
    phase_copy = load(phase_hbm, phase_v, 6)
    modes_copy = load(modes_hbm.at[0, columns_of(own_half), :], modes_v, 7)
    stress_copy = load(stress_hbm, stress_v, 8)

    barrier = pltpu.get_barrier_semaphore()

    def greet(target):
        pl.semaphore_signal(barrier, inc=1, device_id=target, device_id_type=MESH)

    greet(sibling)

    @pl.when(is_mixer)
    def _():
        each(peers - 1, lambda index: greet(device(lax.rem(me + index + 1, peers))))

    @pl.when(jnp.logical_not(is_mixer))
    def _():
        each(mixers, lambda index: greet(device(mixer_of(index // parts, index % parts))))

    def remote(src, dst, index, target):
        return pltpu.make_async_remote_copy(
            src_ref=src,
            dst_ref=dst,
            send_sem=send_sem.at[index],
            recv_sem=recv_sem.at[index],
            device_id=target,
            device_id_type=MESH,
        )

    def send_to(src, dst, index, target):
        @pl.when(target != me)
        def _():
            remote(src, dst, index, device(target)).start()

        @pl.when(target == me)
        def _():
            pltpu.make_async_copy(src, dst, recv_sem.at[index]).start()

    def arrived(ref, index):
        pltpu.make_async_copy(ref, ref, recv_sem.at[index]).wait()

    load_copy.wait()
    other_copy.wait()
    pair_send[...] = jnp.dot(load_v[...], basis_v[0], preferred_element_type=f32).astype(bf16)

    @pl.when(is_mixer)
    def _():
        pl.semaphore_wait(barrier, peers)

    @pl.when(jnp.logical_not(is_mixer))
    def _():
        pl.semaphore_wait(barrier, mixers + 1)

    pair_copy = remote(pair_send, pair_recv, 0, sibling)
    pair_copy.start()
    own_copy.wait()
    product = jnp.dot(load_v[...], basis_v[1], preferred_element_type=f32)
    pair_copy.wait_recv()
    summed = (product + pair_recv[...].astype(f32)).astype(bf16)
    for part in range(parts):
        part_send[part] = summed[:, part * width : (part + 1) * width].reshape(
            groups, ROWS, width
        )
    for part in range(parts):
        for group in range(groups):
            send_to(
                part_send.at[part, group],
                part_recv.at[own_sector, own_pair],
                1,
                mixer_of(group, part),
            )

    slot_copy.wait()
    count_copy.wait()
    decay_copy.wait()
    phase_copy.wait()

    @pl.when(is_mixer)
    def _():
        wide = sectors * ROWS
        row = lax.broadcasted_iota(jnp.int32, (sectors, wide), 0)
        sector = (lax.broadcasted_iota(jnp.int32, (sectors, wide), 1) // ROWS).astype(f32)
        harmonic = jnp.zeros((sectors, wide), f32)
        for slot in range(sectors):
            harmonic = jnp.where(row == slot, slot_s[slot].astype(f32), harmonic)
        middle = float(sectors // 2)
        sine = harmonic > middle
        order = jnp.where(sine, harmonic - middle, harmonic)
        turns = order * sector
        residue = turns - float(sectors) * jnp.floor(turns * (1.0 / sectors))
        angle = residue * jnp.float32(2.0 * math.pi / sectors)
        wave = jnp.cos(angle - jnp.where(sine, jnp.float32(0.5 * math.pi), jnp.float32(0.0)))
        single = (harmonic == 0.0) | (harmonic == middle)
        weight = jnp.where(
            single, jnp.float32(math.sqrt(1.0 / sectors)), jnp.float32(math.sqrt(2.0 / sectors))
        )
        small = weight * wave
        table = jnp.broadcast_to(small[:, None, :], (sectors, ROWS, wide)).reshape(wide, wide)
        left = lax.broadcasted_iota(jnp.int32, (wide, wide), 0) % ROWS
        right = lax.broadcasted_iota(jnp.int32, (wide, wide), 1) % ROWS
        table = jnp.where(left == right, table, 0.0)
        for where_to, values in ((fwd_table, table), (bwd_table, table.T)):
            high = values.astype(bf16)
            where_to[0] = high
            where_to[1] = (values - high.astype(f32)).astype(bf16)

    def mix(table_ref, values):
        return (
            jnp.dot(table_ref[0], values, preferred_element_type=f32)
            + jnp.dot(table_ref[1], values, preferred_element_type=f32)
        ).astype(bf16)

    def spread(source, sink, which):
        dst = sink.at[own_group, :, pl.ds(pl.multiple_of(own_pair * width, 128), width)]

        def send(index):
            target = lax.rem(me + index + 1, peers)
            remote(source.at[target // parts], dst, which, device(target)).start()

        each(peers - 1, send)
        pltpu.make_async_copy(source.at[own_sector], dst, recv_sem.at[which]).start()

    @pl.when(is_mixer)
    def _():
        arrived(part_recv, 1)
        total = part_recv[:, 0].astype(f32)
        for pair in range(1, parts):
            total = total + part_recv[:, pair].astype(f32)
        values = total.reshape(sectors * ROWS, width).astype(bf16)
        spec_send[...] = mix(fwd_table, values).reshape(sectors, ROWS, width)
        spread(spec_send, spec_recv, 2)

    decay = decay_v[...]
    lag = lax.broadcasted_iota(jnp.int32, lag_table.shape, 0).astype(f32)
    gain = jnp.sqrt(1.0 - jnp.exp(-2.0 * decay))
    lag_table[...] = gain * jnp.exp(-decay * lag) * jnp.cos(phase_v[...] * lag)
    padded[pl.ds(0, steps), :] = jnp.zeros((steps, padded.shape[1]), f32)

    modes_copy.wait()
    arrived(spec_recv, 2)
    modal_send[...] = jnp.dot(
        spec_recv[...].reshape(steps, half), modes_v[...], preferred_element_type=f32
    )
    modal_copy = remote(modal_send, modal_recv, 3, sibling)
    modal_copy.start()
    modal_copy.wait_recv()
    modal = modal_send[...] + modal_recv[...]
    mode = lax.broadcasted_iota(jnp.int32, modal.shape, 1)
    padded[pl.ds(steps, steps), :] = jnp.where(mode < count_s[0], modal, 0.0)
    cut = steps // 2
    upper = jnp.zeros((cut, modal.shape[1]), f32)
    lower = jnp.zeros((cut, modal.shape[1]), f32)
    for n in range(steps):
        scale = lag_table[pl.ds(n, 1), :]
        if n < cut:
            upper = upper + scale * padded[pl.ds(steps - n, cut), :]
        lower = lower + scale * padded[pl.ds(steps + cut - n, cut), :]
    response = jnp.concatenate([upper, lower], axis=0).astype(bf16)
    own_rows = modes_v[pl.ds(pl.multiple_of(own_pair * width, 128), width), :]
    returned = lax.dot_general(
        response, own_rows, (((1,), (1,)), ((), ())), preferred_element_type=f32
    )
    ret_send[...] = returned.astype(bf16).reshape(groups, ROWS, width)
    for group in range(groups):
        send_to(ret_send.at[group], ret_recv.at[own_sector], 4, mixer_of(group, own_pair))

    @pl.when(is_mixer)
    def _():
        arrived(ret_recv, 4)
        values = ret_recv[...].reshape(sectors * ROWS, width)
        back_send[...] = mix(bwd_table, values).reshape(sectors, ROWS, width)
        spread(back_send, back_recv, 5)

    stress_copy.wait()
    arrived(back_recv, 5)
    back_copy = remote(back_recv, back_other, 6, sibling)
    back_copy.start()

    def rows_of(which):
        return stress_v[pl.ds(pl.multiple_of(which * half, 128), half), :]

    field = jnp.dot(
        back_recv[...].reshape(steps, half), rows_of(own_half), preferred_element_type=f32
    )
    back_copy.wait_recv()
    field = field + jnp.dot(
        back_other[...].reshape(steps, half), rows_of(other_half), preferred_element_type=f32
    )
    out_ref[0] = field.astype(bf16)

    def sent(ref, index):
        pltpu.make_async_copy(ref, ref, send_sem.at[index]).wait()

    pair_copy.wait_send()
    modal_copy.wait_send()
    back_copy.wait_send()

    @pl.when(is_mixer)
    def _():
        for part in range(parts):
            sent(part_send.at[part, pl.ds(0, groups - (part == 0))], 1)
        for index in (2, 5):
            sent(part_recv.at[pl.ds(0, sectors - 1)], index)
            if parts > 1:
                sent(part_recv.at[0, pl.ds(0, parts - 1)], index)
        sent(ret_send.at[pl.ds(0, groups - 1)], 4)

    @pl.when(jnp.logical_not(is_mixer))
    def _():
        sent(part_send, 1)
        sent(ret_send, 4)


def local(
    sectors,
    dofs,
    load_history,
    sector_basis,
    harmonic_modes,
    stress_basis,
    mode_decay,
    mode_phase,
    mode_count,
    slot_harmonic,
):
    _, steps, rows = load_history.shape
    reduced = sector_basis.shape[1]
    modes = harmonic_modes.shape[2]
    stress = stress_basis.shape[1]
    width = reduced // dofs
    groups = steps // ROWS
    parts = dofs // HALVES
    half = reduced // HALVES
    wide = sectors * ROWS
    bf16, f32 = jnp.bfloat16, jnp.float32
    flops = 2 * steps * reduced * (rows + stress + 2 * modes)
    return pl.pallas_call(
        functools.partial(kernel, sectors, dofs),
        out_shape=jax.ShapeDtypeStruct((1, steps, stress), bf16),
        in_specs=[pl.BlockSpec(memory_space=pltpu.HBM)] * 8,
        out_specs=pl.BlockSpec(memory_space=pltpu.VMEM),
        scratch_shapes=[
            pltpu.VMEM((steps, rows), bf16),
            pltpu.VMEM((HALVES, rows, half), bf16),
            pltpu.VMEM((half, modes), bf16),
            pltpu.VMEM((reduced, stress), bf16),
            pltpu.VMEM(mode_decay.shape, f32),
            pltpu.VMEM(mode_phase.shape, f32),
            pltpu.SMEM(mode_count.shape, jnp.int32),
            pltpu.SMEM(slot_harmonic.shape, jnp.int32),
            pltpu.VMEM((steps, half), bf16),
            pltpu.VMEM((steps, half), bf16),
            pltpu.VMEM((parts, groups, ROWS, width), bf16),
            pltpu.VMEM((sectors, parts, ROWS, width), bf16),
            pltpu.VMEM((sectors, ROWS, width), bf16),
            pltpu.VMEM((groups, ROWS, half), bf16),
            pltpu.VMEM((steps, modes), f32),
            pltpu.VMEM((steps, modes), f32),
            pltpu.VMEM((groups, ROWS, width), bf16),
            pltpu.VMEM((sectors, ROWS, width), bf16),
            pltpu.VMEM((sectors, ROWS, width), bf16),
            pltpu.VMEM((groups, ROWS, half), bf16),
            pltpu.VMEM((groups, ROWS, half), bf16),
            pltpu.VMEM((2, wide, wide), bf16),
            pltpu.VMEM((2, wide, wide), bf16),
            pltpu.VMEM((steps, modes), f32),
            pltpu.VMEM((2 * steps, modes), f32),
            pltpu.SemaphoreType.DMA((9,)),
            pltpu.SemaphoreType.DMA((7,)),
            pltpu.SemaphoreType.DMA((7,)),
        ],
        compiler_params=pltpu.CompilerParams(
            collective_id=0, has_side_effects=True, vmem_limit_bytes=60 * 1024 * 1024
        ),
        cost_estimate=pl.CostEstimate(
            flops=flops, bytes_accessed=2 * reduced * (rows + stress), transcendentals=0
        ),
    )(
        load_history,
        sector_basis,
        harmonic_modes,
        stress_basis,
        mode_decay,
        mode_phase,
        mode_count,
        slot_harmonic,
    )


def solution(mesh):
    return jax.shard_map(
        functools.partial(local, mesh.shape["sector"], mesh.shape["dof"]),
        mesh=mesh,
        in_specs=(
            P("sector", None, "dof"),
            P("dof", None),
            P("sector", None, None),
            P(None, "dof"),
            P("sector", None),
            P("sector", None),
            P("sector"),
            P(),
        ),
        out_specs=P("sector", None, "dof"),
        check_vma=False,
    )
```

time: 40.5 us -> 32.7 us (0.81)
  local copies, waits for them, and re-layouts: 7.08 us -> 1.62 us
  Pallas kernels: 32.2 us -> 30.2 us
    unnamed x13 -> x1, local copies, waits for them, and re-layouts: 7.08 us -> 1.62 us
    pallas_call x1, Pallas kernels: 32.2 us -> 30.2 us  [local(): pl.pallas_call(functools.partial(kernel, sectors, dofs), out_shape=jax.Sh...]
where the time goes in v2:
time: 32.7 us; the launch traced here: 32.5 us
  Pallas kernels  30.2 us (92%)
  local copies, waits for them, and re-layouts  1.62 us (5%)
  between operations  0.66 us (2%)
    pallas_call x1, Pallas kernels, local(): pl.pallas_call(functools.partial(kernel, sectors, dofs), out_shape=jax.Sh...  30.2 us
    unnamed x1, local copies, waits for them, and re-layouts  1.62 us

profile of v2, /device:TPU:1, one launch (start us, length us, event | category | flops | bytes accessed | tf_op | source)
XLA Modules:
  0.0 32.5 jit_solution(11479441246121412741)
XLA Ops:
  0.7 30.2 %shard_map.82 = bf16[1,64,1536]{2,1,0:T(8,128)(2,1)} custom-call(bf16[1,64,1536]{2,1,0:T(8,128)(2,1)} %load_hbm.1, bf16[1536,1536]{1,0:T(8,128)(2,1)} %basis_hbm.1, bf16[1,1536,256]{2,1,0:T(8,128)(2,1)} %modes_hbm.1, bf16[1536,1536]{1,0:T(8,128)(2,1)} %stress_hbm.1, f32[1,256]{1,0:T(1,128)} %decay_hbm.1, f32[1,256]{1,0:T(1,128)} %phase_hbm.1, ...), custom_call_target="tpu_custom_call" | custom-call | flops 704643072 | bytes 9437184 | tf_op jit(solution)/shard_map/pallas_call | solution.py:345
  30.9 1.6 %copy.11 = bf16[1,64,1536]{2,1,0:T(8,128)(2,1)} copy(bf16[1,64,1536]{2,1,0:T(8,128)(2,1)} %shard_map.82) | data formatting | bytes 393216

commit v3 on v2

--- a/solution.py
+++ b/solution.py
@@ -11,6 +11,7 @@
 MESH = pl.DeviceIdType.MESH
 ROWS = 16
 HALVES = 2
+CHUNKS = 3
 
 
 def each(count, body):
@@ -59,8 +60,8 @@
     back_other,
     fwd_table,
     bwd_table,
-    lag_table,
-    padded,
+    power_real,
+    power_imag,
     local_sem,
     send_sem,
     recv_sem,
@@ -101,14 +102,27 @@
         return pl.ds(pl.multiple_of(which * half, 128), half)
 
     load_copy = load(load_hbm.at[0], load_v, 0)
-    other_copy = load(basis_hbm.at[:, columns_of(other_half)], basis_v.at[0], 1)
-    own_copy = load(basis_hbm.at[:, columns_of(own_half)], basis_v.at[1], 2)
-    slot_copy = load(slot_hbm, slot_s, 3)
-    count_copy = load(count_hbm, count_s, 4)
-    decay_copy = load(decay_hbm, decay_v, 5)
-    phase_copy = load(phase_hbm, phase_v, 6)
-    modes_copy = load(modes_hbm.at[0, columns_of(own_half), :], modes_v, 7)
-    stress_copy = load(stress_hbm, stress_v, 8)
+    chunk = load_v.shape[1] // CHUNKS
+    basis_copies = [
+        [
+            load(
+                basis_hbm.at[pl.ds(index * chunk, chunk), columns_of(which)],
+                basis_v.at[turn, pl.ds(index * chunk, chunk)],
+                7 + turn * CHUNKS + index,
+            )
+            for index in range(CHUNKS)
+        ]
+        for turn, which in enumerate((other_half, own_half))
+    ]
+
+    def partial_product(turn):
+        total = None
+        for index in range(CHUNKS):
+            rows = pl.ds(index * chunk, chunk)
+            basis_copies[turn][index].wait()
+            term = jnp.dot(load_v[:, rows], basis_v[turn, rows, :], preferred_element_type=f32)
+            total = term if total is None else total + term
+        return total
 
     barrier = pltpu.get_barrier_semaphore()
 
@@ -148,8 +162,7 @@
         pltpu.make_async_copy(ref, ref, recv_sem.at[index]).wait()
 
     load_copy.wait()
-    other_copy.wait()
-    pair_send[...] = jnp.dot(load_v[...], basis_v[0], preferred_element_type=f32).astype(bf16)
+    pair_send[...] = partial_product(0).astype(bf16)
 
     @pl.when(is_mixer)
     def _():
@@ -161,8 +174,13 @@
 
     pair_copy = remote(pair_send, pair_recv, 0, sibling)
     pair_copy.start()
-    own_copy.wait()
-    product = jnp.dot(load_v[...], basis_v[1], preferred_element_type=f32)
+    product = partial_product(1)
+    slot_copy = load(slot_hbm, slot_s, 1)
+    count_copy = load(count_hbm, count_s, 2)
+    decay_copy = load(decay_hbm, decay_v, 3)
+    phase_copy = load(phase_hbm, phase_v, 4)
+    modes_copy = load(modes_hbm.at[0, columns_of(own_half), :], modes_v, 5)
+    stress_copy = load(stress_hbm, stress_v, 6)
     pair_copy.wait_recv()
     summed = (product + pair_recv[...].astype(f32)).astype(bf16)
     for part in range(parts):
@@ -239,10 +257,11 @@
         spread(spec_send, spec_recv, 2)
 
     decay = decay_v[...]
-    lag = lax.broadcasted_iota(jnp.int32, lag_table.shape, 0).astype(f32)
     gain = jnp.sqrt(1.0 - jnp.exp(-2.0 * decay))
-    lag_table[...] = gain * jnp.exp(-decay * lag) * jnp.cos(phase_v[...] * lag)
-    padded[pl.ds(0, steps), :] = jnp.zeros((steps, padded.shape[1]), f32)
+    power = lax.shift_left(1, lax.broadcasted_iota(jnp.int32, power_real.shape, 0)).astype(f32)
+    damping = jnp.exp(-decay * power)
+    power_real[...] = damping * jnp.cos(phase_v[...] * power)
+    power_imag[...] = damping * jnp.sin(phase_v[...] * power)
 
     modes_copy.wait()
     arrived(spec_recv, 2)
@@ -254,16 +273,27 @@
     modal_copy.wait_recv()
     modal = modal_send[...] + modal_recv[...]
     mode = lax.broadcasted_iota(jnp.int32, modal.shape, 1)
-    padded[pl.ds(steps, steps), :] = jnp.where(mode < count_s[0], modal, 0.0)
-    cut = steps // 2
-    upper = jnp.zeros((cut, modal.shape[1]), f32)
-    lower = jnp.zeros((cut, modal.shape[1]), f32)
-    for n in range(steps):
-        scale = lag_table[pl.ds(n, 1), :]
-        if n < cut:
-            upper = upper + scale * padded[pl.ds(steps - n, cut), :]
-        lower = lower + scale * padded[pl.ds(steps + cut - n, cut), :]
-    response = jnp.concatenate([upper, lower], axis=0).astype(bf16)
+    real = jnp.where(mode < count_s[0], modal, 0.0)
+    imag = None
+    step = lax.broadcasted_iota(jnp.int32, modal.shape, 0)
+
+    def later(values, lag):
+        if lag % 8 == 0:
+            zeros = jnp.zeros((lag, values.shape[1]), f32)
+            return jnp.concatenate([zeros, values[: steps - lag]], axis=0)
+        return jnp.where(step >= lag, pltpu.roll(values, lag, 0), 0.0)
+
+    for index in range((steps - 1).bit_length()):
+        turn_real, turn_imag = power_real[pl.ds(index, 1), :], power_imag[pl.ds(index, 1), :]
+        old_real = later(real, 1 << index)
+        if imag is None:
+            imag = turn_imag * old_real
+            real = real + turn_real * old_real
+        else:
+            old_imag = later(imag, 1 << index)
+            real = real + turn_real * old_real - turn_imag * old_imag
+            imag = imag + turn_real * old_imag + turn_imag * old_real
+    response = (gain * real).astype(bf16)
     own_rows = modes_v[pl.ds(pl.multiple_of(own_pair * width, 128), width), :]
     returned = lax.dot_general(
         response, own_rows, (((1,), (1,)), ((), ())), preferred_element_type=f32
@@ -294,7 +324,7 @@
     field = field + jnp.dot(
         back_other[...].reshape(steps, half), rows_of(other_half), preferred_element_type=f32
     )
-    out_ref[0] = field.astype(bf16)
+    out_ref[0] = field
 
     def sent(ref, index):
         pltpu.make_async_copy(ref, ref, send_sem.at[index]).wait()
@@ -342,9 +372,9 @@
     wide = sectors * ROWS
     bf16, f32 = jnp.bfloat16, jnp.float32
     flops = 2 * steps * reduced * (rows + stress + 2 * modes)
-    return pl.pallas_call(
+    field = pl.pallas_call(
         functools.partial(kernel, sectors, dofs),
-        out_shape=jax.ShapeDtypeStruct((1, steps, stress), bf16),
+        out_shape=jax.ShapeDtypeStruct((1, steps, stress), f32),
         in_specs=[pl.BlockSpec(memory_space=pltpu.HBM)] * 8,
         out_specs=pl.BlockSpec(memory_space=pltpu.VMEM),
         scratch_shapes=[
@@ -371,9 +401,9 @@
             pltpu.VMEM((groups, ROWS, half), bf16),
             pltpu.VMEM((2, wide, wide), bf16),
             pltpu.VMEM((2, wide, wide), bf16),
-            pltpu.VMEM((steps, modes), f32),
-            pltpu.VMEM((2 * steps, modes), f32),
-            pltpu.SemaphoreType.DMA((9,)),
+            pltpu.VMEM((8, modes), f32),
+            pltpu.VMEM((8, modes), f32),
+            pltpu.SemaphoreType.DMA((7 + HALVES * CHUNKS,)),
             pltpu.SemaphoreType.DMA((7,)),
             pltpu.SemaphoreType.DMA((7,)),
         ],
@@ -393,6 +423,7 @@
         mode_count,
         slot_harmonic,
     )
+    return field.astype(bf16)
 
 
 def solution(mesh):

time: 32.7 us -> 32.2 us (0.985)
  other arithmetic: 0 us -> 1.69 us
  local copies, waits for them, and re-layouts: 1.62 us -> 0 us
  Pallas kernels: 30.2 us -> 29.7 us
    convert_element_type x0 -> x1, other arithmetic: none -> 1.69 us  [local(): return field.astype(bf16)]
    unnamed x1 -> x0, local copies, waits for them, and re-layouts: 1.62 us -> none
    pallas_call x1, Pallas kernels: 30.2 us -> 29.7 us  [local(): pl.pallas_call(functools.partial(kernel, sectors, dofs), out_shape=jax.Sh...]
where the time goes in v3:
time: 32.2 us; the launch traced here: 32 us
  Pallas kernels  29.7 us (92%)
  other arithmetic  1.69 us (5%)
  between operations  0.66 us (2%)
    pallas_call x1, Pallas kernels, local(): pl.pallas_call(functools.partial(kernel, sectors, dofs), out_shape=jax.Sh...  29.7 us
    convert_element_type x1, other arithmetic, local(): return field.astype(bf16)  1.69 us

profile of v3, /device:TPU:1, one launch (start us, length us, event | category | flops | bytes accessed | tf_op | source)
XLA Modules:
  0.0 32.0 jit_solution(9475827960091250865)
XLA Ops:
  0.7 29.7 %shard_map.82 = f32[1,64,1536]{2,1,0:T(8,128)} custom-call(bf16[1,64,1536]{2,1,0:T(8,128)(2,1)} %load_hbm.1, bf16[1536,1536]{1,0:T(8,128)(2,1)} %basis_hbm.1, bf16[1,1536,256]{2,1,0:T(8,128)(2,1)} %modes_hbm.1, bf16[1536,1536]{1,0:T(8,128)(2,1)} %stress_hbm.1, f32[1,256]{1,0:T(1,128)} %decay_hbm.1, f32[1,256]{1,0:T(1,128)} %phase_hbm.1, ...), custom_call_target="tpu_custom_call" | custom-call | flops 704643072 | bytes 9437184 | tf_op jit(solution)/shard_map/pallas_call | solution.py:375
  30.3 1.7 %convert_element_type.3 = bf16[1,64,1536]{2,1,0:T(8,128)(2,1)} convert(f32[1,64,1536]{2,1,0:T(8,128)} %shard_map.82) | non-fusion elementwise | flops 98304 | bytes 589824 | tf_op jit(solution)/shard_map/convert_element_type | solution.py:426

commit v4 on v3

--- a/solution.py
+++ b/solution.py
@@ -11,6 +11,7 @@
 MESH = pl.DeviceIdType.MESH
 ROWS = 16
 HALVES = 2
+HEAD = 8
 CHUNKS = 3
 
 
@@ -32,19 +33,12 @@
     basis_hbm,
     modes_hbm,
     stress_hbm,
-    decay_hbm,
-    phase_hbm,
-    count_hbm,
-    slot_hbm,
+    small_ref,
     out_ref,
     load_v,
     basis_v,
     modes_v,
     stress_v,
-    decay_v,
-    phase_v,
-    count_s,
-    slot_s,
     pair_send,
     pair_recv,
     part_send,
@@ -108,7 +102,7 @@
             load(
                 basis_hbm.at[pl.ds(index * chunk, chunk), columns_of(which)],
                 basis_v.at[turn, pl.ds(index * chunk, chunk)],
-                7 + turn * CHUNKS + index,
+                3 + turn * CHUNKS + index,
             )
             for index in range(CHUNKS)
         ]
@@ -161,6 +155,40 @@
     def arrived(ref, index):
         pltpu.make_async_copy(ref, ref, recv_sem.at[index]).wait()
 
+    @pl.when(is_mixer)
+    def _():
+        wide = sectors * ROWS
+        sector = (lax.broadcasted_iota(jnp.int32, (sectors, wide), 1) >> (ROWS.bit_length() - 1)).astype(f32)
+        harmonic = jnp.broadcast_to(small_ref[pl.ds(HEAD, sectors), 0:1], (sectors, wide))
+        middle = float(sectors // 2)
+        sine = harmonic > middle
+        order = jnp.where(sine, harmonic - middle, harmonic)
+        turns = order * sector
+        residue = turns - float(sectors) * jnp.floor(turns * (1.0 / sectors))
+        angle = residue * jnp.float32(2.0 * math.pi / sectors)
+        wave = jnp.cos(angle - jnp.where(sine, jnp.float32(0.5 * math.pi), jnp.float32(0.0)))
+        single = (harmonic == 0.0) | (harmonic == middle)
+        weight = jnp.where(
+            single, jnp.float32(math.sqrt(1.0 / sectors)), jnp.float32(math.sqrt(2.0 / sectors))
+        )
+        small = weight * wave
+        table = jnp.broadcast_to(small[:, None, :], (sectors, ROWS, wide)).reshape(wide, wide)
+        left = lax.broadcasted_iota(jnp.int32, (wide, wide), 0) & (ROWS - 1)
+        right = lax.broadcasted_iota(jnp.int32, (wide, wide), 1) & (ROWS - 1)
+        table = jnp.where(left == right, table, 0.0)
+        for where_to, values in ((fwd_table, table), (bwd_table, table.T)):
+            high = values.astype(bf16)
+            where_to[0] = high
+            where_to[1] = (values - high.astype(f32)).astype(bf16)
+
+    decay = small_ref[0:1, :]
+    phase = small_ref[1:2, :]
+    gain = jnp.sqrt(1.0 - jnp.exp(-2.0 * decay))
+    power = lax.shift_left(1, lax.broadcasted_iota(jnp.int32, power_real.shape, 0)).astype(f32)
+    damping = jnp.exp(-decay * power)
+    power_real[...] = damping * jnp.cos(phase * power)
+    power_imag[...] = damping * jnp.sin(phase * power)
+
     load_copy.wait()
     pair_send[...] = partial_product(0).astype(bf16)
 
@@ -175,12 +203,8 @@
     pair_copy = remote(pair_send, pair_recv, 0, sibling)
     pair_copy.start()
     product = partial_product(1)
-    slot_copy = load(slot_hbm, slot_s, 1)
-    count_copy = load(count_hbm, count_s, 2)
-    decay_copy = load(decay_hbm, decay_v, 3)
-    phase_copy = load(phase_hbm, phase_v, 4)
-    modes_copy = load(modes_hbm.at[0, columns_of(own_half), :], modes_v, 5)
-    stress_copy = load(stress_hbm, stress_v, 6)
+    modes_copy = load(modes_hbm.at[0, columns_of(own_half), :], modes_v, 1)
+    stress_copy = load(stress_hbm, stress_v, 2)
     pair_copy.wait_recv()
     summed = (product + pair_recv[...].astype(f32)).astype(bf16)
     for part in range(parts):
@@ -196,40 +220,6 @@
                 mixer_of(group, part),
             )
 
-    slot_copy.wait()
-    count_copy.wait()
-    decay_copy.wait()
-    phase_copy.wait()
-
-    @pl.when(is_mixer)
-    def _():
-        wide = sectors * ROWS
-        row = lax.broadcasted_iota(jnp.int32, (sectors, wide), 0)
-        sector = (lax.broadcasted_iota(jnp.int32, (sectors, wide), 1) // ROWS).astype(f32)
-        harmonic = jnp.zeros((sectors, wide), f32)
-        for slot in range(sectors):
-            harmonic = jnp.where(row == slot, slot_s[slot].astype(f32), harmonic)
-        middle = float(sectors // 2)
-        sine = harmonic > middle
-        order = jnp.where(sine, harmonic - middle, harmonic)
-        turns = order * sector
-        residue = turns - float(sectors) * jnp.floor(turns * (1.0 / sectors))
-        angle = residue * jnp.float32(2.0 * math.pi / sectors)
-        wave = jnp.cos(angle - jnp.where(sine, jnp.float32(0.5 * math.pi), jnp.float32(0.0)))
-        single = (harmonic == 0.0) | (harmonic == middle)
-        weight = jnp.where(
-            single, jnp.float32(math.sqrt(1.0 / sectors)), jnp.float32(math.sqrt(2.0 / sectors))
-        )
-        small = weight * wave
-        table = jnp.broadcast_to(small[:, None, :], (sectors, ROWS, wide)).reshape(wide, wide)
-        left = lax.broadcasted_iota(jnp.int32, (wide, wide), 0) % ROWS
-        right = lax.broadcasted_iota(jnp.int32, (wide, wide), 1) % ROWS
-        table = jnp.where(left == right, table, 0.0)
-        for where_to, values in ((fwd_table, table), (bwd_table, table.T)):
-            high = values.astype(bf16)
-            where_to[0] = high
-            where_to[1] = (values - high.astype(f32)).astype(bf16)
-
     def mix(table_ref, values):
         return (
             jnp.dot(table_ref[0], values, preferred_element_type=f32)
@@ -256,13 +246,6 @@
         spec_send[...] = mix(fwd_table, values).reshape(sectors, ROWS, width)
         spread(spec_send, spec_recv, 2)
 
-    decay = decay_v[...]
-    gain = jnp.sqrt(1.0 - jnp.exp(-2.0 * decay))
-    power = lax.shift_left(1, lax.broadcasted_iota(jnp.int32, power_real.shape, 0)).astype(f32)
-    damping = jnp.exp(-decay * power)
-    power_real[...] = damping * jnp.cos(phase_v[...] * power)
-    power_imag[...] = damping * jnp.sin(phase_v[...] * power)
-
     modes_copy.wait()
     arrived(spec_recv, 2)
     modal_send[...] = jnp.dot(
@@ -272,8 +255,8 @@
     modal_copy.start()
     modal_copy.wait_recv()
     modal = modal_send[...] + modal_recv[...]
-    mode = lax.broadcasted_iota(jnp.int32, modal.shape, 1)
-    real = jnp.where(mode < count_s[0], modal, 0.0)
+    mode = lax.broadcasted_iota(jnp.int32, modal.shape, 1).astype(f32)
+    real = jnp.where(mode < small_ref[2:3, :], modal, 0.0)
     imag = None
     step = lax.broadcasted_iota(jnp.int32, modal.shape, 0)
 
@@ -324,7 +307,7 @@
     field = field + jnp.dot(
         back_other[...].reshape(steps, half), rows_of(other_half), preferred_element_type=f32
     )
-    out_ref[0] = field
+    out_ref[0] = field.astype(bf16)
 
     def sent(ref, index):
         pltpu.make_async_copy(ref, ref, send_sem.at[index]).wait()
@@ -371,21 +354,23 @@
     half = reduced // HALVES
     wide = sectors * ROWS
     bf16, f32 = jnp.bfloat16, jnp.float32
+    row = jnp.arange(HEAD + sectors, dtype=jnp.int32)[:, None]
+    numbers = jnp.where(row == 2, mode_count[0], jnp.pad(slot_harmonic, (HEAD, 0))[:, None])
+    small = jnp.where(
+        row == 0, mode_decay, jnp.where(row == 1, mode_phase, numbers.astype(f32))
+    )
     flops = 2 * steps * reduced * (rows + stress + 2 * modes)
-    field = pl.pallas_call(
+    return pl.pallas_call(
         functools.partial(kernel, sectors, dofs),
-        out_shape=jax.ShapeDtypeStruct((1, steps, stress), f32),
-        in_specs=[pl.BlockSpec(memory_space=pltpu.HBM)] * 8,
+        out_shape=jax.ShapeDtypeStruct((1, steps, stress), bf16),
+        in_specs=[pl.BlockSpec(memory_space=pltpu.HBM)] * 4
+        + [pl.BlockSpec(memory_space=pltpu.VMEM)],
         out_specs=pl.BlockSpec(memory_space=pltpu.VMEM),
         scratch_shapes=[
             pltpu.VMEM((steps, rows), bf16),
             pltpu.VMEM((HALVES, rows, half), bf16),
             pltpu.VMEM((half, modes), bf16),
             pltpu.VMEM((reduced, stress), bf16),
-            pltpu.VMEM(mode_decay.shape, f32),
-            pltpu.VMEM(mode_phase.shape, f32),
-            pltpu.SMEM(mode_count.shape, jnp.int32),
-            pltpu.SMEM(slot_harmonic.shape, jnp.int32),
             pltpu.VMEM((steps, half), bf16),
             pltpu.VMEM((steps, half), bf16),
             pltpu.VMEM((parts, groups, ROWS, width), bf16),
@@ -403,12 +388,12 @@
             pltpu.VMEM((2, wide, wide), bf16),
             pltpu.VMEM((8, modes), f32),
             pltpu.VMEM((8, modes), f32),
-            pltpu.SemaphoreType.DMA((7 + HALVES * CHUNKS,)),
+            pltpu.SemaphoreType.DMA((3 + HALVES * CHUNKS,)),
             pltpu.SemaphoreType.DMA((7,)),
             pltpu.SemaphoreType.DMA((7,)),
         ],
         compiler_params=pltpu.CompilerParams(
-            collective_id=0, has_side_effects=True, vmem_limit_bytes=60 * 1024 * 1024
+            collective_id=0, has_side_effects=True, vmem_limit_bytes=54980 * 1024
         ),
         cost_estimate=pl.CostEstimate(
             flops=flops, bytes_accessed=2 * reduced * (rows + stress), transcendentals=0
@@ -418,12 +403,8 @@
         sector_basis,
         harmonic_modes,
         stress_basis,
-        mode_decay,
-        mode_phase,
-        mode_count,
-        slot_harmonic,
-    )
-    return field.astype(bf16)
+        small,
+    )
 
 
 def solution(mesh):

time: 32.2 us -> 31.9 us (level)
  Pallas kernels: 29.7 us -> 28.9 us
  local copies, waits for them, and re-layouts: 0 us -> 0.68 us
    convert_element_type x1, other arithmetic: 1.69 us -> 0.73 us  [local(): numbers.astype(f32)]
    pallas_call x1, Pallas kernels: 29.7 us -> 28.9 us  [local(): pl.pallas_call(functools.partial(kernel, sectors, dofs), out_shape=jax.Sh...]
    select_n x0 -> x1, other arithmetic: none -> 0.77 us  [local(): jnp.where(row == 0, mode_decay, jnp.where(row == 1, mode_phase, numbers.a...]
    unnamed x0 -> x1, local copies, waits for them, and re-layouts: none -> 0.68 us
where the time goes in v4:
time: 31.9 us; the launch traced here: 31.7 us
  Pallas kernels  28.9 us (91%)
  other arithmetic  1.5 us (5%)
  local copies, waits for them, and re-layouts  0.68 us (2%)
  between operations  0.66 us (2%)
    pallas_call x1, Pallas kernels, local(): pl.pallas_call(functools.partial(kernel, sectors, dofs), out_shape=jax.Sh...  28.9 us
    select_n x1, other arithmetic, local(): jnp.where(row == 0, mode_decay, jnp.where(row == 1, mode_phase, numbers.a...  0.77 us
    convert_element_type x1, other arithmetic, local(): numbers.astype(f32)  0.73 us
    unnamed x1, local copies, waits for them, and re-layouts  0.68 us

profile of v4, /device:TPU:1, one launch (start us, length us, event | category | flops | bytes accessed | tf_op | source)
XLA Modules:
  0.0 31.7 jit_solution(1340388425648052289)
XLA Ops:
  0.7 0.7 %fusion = f32[16]{0:T(128)S(1)} fusion(s32[8]{0:T(128)} %param.15, s32[]{:T(128)} %bitcast.3), kind=kLoop, calls=%fused_computation.2 | loop fusion | flops 48 | bytes 100 | tf_op jit(solution)/shard_map/convert_element_type | solution.py:360
  1.4 0.8 %select_select_fusion.small_ref = f32[16,256]{1,0:T(8,128)S(1)} fusion(f32[16]{0:T(128)S(1)} %fusion, f32[256]{0:T(256)} %bitcast.4, f32[256]{0:T(256)} %bitcast.5, pred[16]{0:T(512)(128)(4,1)S(1)} %get-tuple-element.5, pred[16]{0:T(512)(128)(4,1)S(1)} %get-tuple-element.6), kind=kLoop, calls=%fused_computation | loop fusion | flops 8192 | bytes 18528 | tf_op jit(solution)/shard_map/jit(_where)/select_n | solution.py:359
  2.2 28.9 %shard_map.82 = bf16[1,64,1536]{2,1,0:T(8,128)(2,1)S(1)} custom-call(bf16[1,64,1536]{2,1,0:T(8,128)(2,1)} %load_hbm.1, bf16[1536,1536]{1,0:T(8,128)(2,1)} %basis_hbm.1, bf16[1,1536,256]{2,1,0:T(8,128)(2,1)} %modes_hbm.1, bf16[1536,1536]{1,0:T(8,128)(2,1)} %stress_hbm.1, f32[16,256]{1,0:T(8,128)S(1)} %select_select_fusion.small_ref), custom_call_target="tpu_custom_call" | custom-call | flops 704643072 | bytes 9437184 | tf_op jit(solution)/shard_map/pallas_call | solution.py:363
  31.1 0.7 %copy.11 = bf16[1,64,1536]{2,1,0:T(8,128)(2,1)} copy(bf16[1,64,1536]{2,1,0:T(8,128)(2,1)S(1)} %shard_map.82) | data formatting | bytes 393216
  (1 shorter events, 0.0 us)

commit v5 on v4

--- a/solution.py
+++ b/solution.py
@@ -11,7 +11,6 @@
 MESH = pl.DeviceIdType.MESH
 ROWS = 16
 HALVES = 2
-HEAD = 8
 CHUNKS = 3
 
 
@@ -24,6 +23,10 @@
         @pl.loop(0, count)
         def _(index):
             body(index)
+
+
+def farthest_first(count):
+    return sorted(range(count), key=lambda offset: -min(offset, count - offset))
 
 
 def kernel(
@@ -33,12 +36,19 @@
     basis_hbm,
     modes_hbm,
     stress_hbm,
-    small_ref,
+    decay_hbm,
+    phase_hbm,
+    count_hbm,
+    slot_hbm,
     out_ref,
     load_v,
     basis_v,
     modes_v,
     stress_v,
+    decay_v,
+    phase_v,
+    count_s,
+    slot_s,
     pair_send,
     pair_recv,
     part_send,
@@ -95,6 +105,10 @@
     def columns_of(which):
         return pl.ds(pl.multiple_of(which * half, 128), half)
 
+    slot_copy = load(slot_hbm, slot_s, 1)
+    count_copy = load(count_hbm, count_s, 2)
+    decay_copy = load(decay_hbm, decay_v, 3)
+    phase_copy = load(phase_hbm, phase_v, 4)
     load_copy = load(load_hbm.at[0], load_v, 0)
     chunk = load_v.shape[1] // CHUNKS
     basis_copies = [
@@ -102,7 +116,7 @@
             load(
                 basis_hbm.at[pl.ds(index * chunk, chunk), columns_of(which)],
                 basis_v.at[turn, pl.ds(index * chunk, chunk)],
-                3 + turn * CHUNKS + index,
+                7 + turn * CHUNKS + index,
             )
             for index in range(CHUNKS)
         ]
@@ -155,11 +169,19 @@
     def arrived(ref, index):
         pltpu.make_async_copy(ref, ref, recv_sem.at[index]).wait()
 
+    slot_copy.wait()
+    count_copy.wait()
+    decay_copy.wait()
+    phase_copy.wait()
+
     @pl.when(is_mixer)
     def _():
         wide = sectors * ROWS
+        row = lax.broadcasted_iota(jnp.int32, (sectors, wide), 0)
         sector = (lax.broadcasted_iota(jnp.int32, (sectors, wide), 1) >> (ROWS.bit_length() - 1)).astype(f32)
-        harmonic = jnp.broadcast_to(small_ref[pl.ds(HEAD, sectors), 0:1], (sectors, wide))
+        harmonic = jnp.zeros((sectors, wide), f32)
+        for slot in range(sectors):
+            harmonic = jnp.where(row == slot, slot_s[slot].astype(f32), harmonic)
         middle = float(sectors // 2)
         sine = harmonic > middle
         order = jnp.where(sine, harmonic - middle, harmonic)
@@ -181,13 +203,12 @@
             where_to[0] = high
             where_to[1] = (values - high.astype(f32)).astype(bf16)
 
-    decay = small_ref[0:1, :]
-    phase = small_ref[1:2, :]
+    decay = decay_v[...]
     gain = jnp.sqrt(1.0 - jnp.exp(-2.0 * decay))
     power = lax.shift_left(1, lax.broadcasted_iota(jnp.int32, power_real.shape, 0)).astype(f32)
     damping = jnp.exp(-decay * power)
-    power_real[...] = damping * jnp.cos(phase * power)
-    power_imag[...] = damping * jnp.sin(phase * power)
+    power_real[...] = damping * jnp.cos(phase_v[...] * power)
+    power_imag[...] = damping * jnp.sin(phase_v[...] * power)
 
     load_copy.wait()
     pair_send[...] = partial_product(0).astype(bf16)
@@ -203,16 +224,17 @@
     pair_copy = remote(pair_send, pair_recv, 0, sibling)
     pair_copy.start()
     product = partial_product(1)
-    modes_copy = load(modes_hbm.at[0, columns_of(own_half), :], modes_v, 1)
-    stress_copy = load(stress_hbm, stress_v, 2)
+    modes_copy = load(modes_hbm.at[0, columns_of(own_half), :], modes_v, 5)
+    stress_copy = load(stress_hbm, stress_v, 6)
     pair_copy.wait_recv()
     summed = (product + pair_recv[...].astype(f32)).astype(bf16)
     for part in range(parts):
         part_send[part] = summed[:, part * width : (part + 1) * width].reshape(
             groups, ROWS, width
         )
-    for part in range(parts):
-        for group in range(groups):
+    for offset in farthest_first(groups):
+        group = lax.rem(own_group + offset, groups)
+        for part in range(parts):
             send_to(
                 part_send.at[part, group],
                 part_recv.at[own_sector, own_pair],
@@ -230,7 +252,8 @@
         dst = sink.at[own_group, :, pl.ds(pl.multiple_of(own_pair * width, 128), width)]
 
         def send(index):
-            target = lax.rem(me + index + 1, peers)
+            swing = (index + 1) // 2
+            target = lax.rem(me + peers // 2 + (1 - index % 2 * 2) * swing, peers)
             remote(source.at[target // parts], dst, which, device(target)).start()
 
         each(peers - 1, send)
@@ -255,8 +278,8 @@
     modal_copy.start()
     modal_copy.wait_recv()
     modal = modal_send[...] + modal_recv[...]
-    mode = lax.broadcasted_iota(jnp.int32, modal.shape, 1).astype(f32)
-    real = jnp.where(mode < small_ref[2:3, :], modal, 0.0)
+    mode = lax.broadcasted_iota(jnp.int32, modal.shape, 1)
+    real = jnp.where(mode < count_s[0, 0], modal, 0.0)
     imag = None
     step = lax.broadcasted_iota(jnp.int32, modal.shape, 0)
 
@@ -282,7 +305,8 @@
         response, own_rows, (((1,), (1,)), ((), ())), preferred_element_type=f32
     )
     ret_send[...] = returned.astype(bf16).reshape(groups, ROWS, width)
-    for group in range(groups):
+    for offset in farthest_first(groups):
+        group = lax.rem(own_group + offset, groups)
         send_to(ret_send.at[group], ret_recv.at[own_sector], 4, mixer_of(group, own_pair))
 
     @pl.when(is_mixer)
@@ -354,23 +378,21 @@
     half = reduced // HALVES
     wide = sectors * ROWS
     bf16, f32 = jnp.bfloat16, jnp.float32
-    row = jnp.arange(HEAD + sectors, dtype=jnp.int32)[:, None]
-    numbers = jnp.where(row == 2, mode_count[0], jnp.pad(slot_harmonic, (HEAD, 0))[:, None])
-    small = jnp.where(
-        row == 0, mode_decay, jnp.where(row == 1, mode_phase, numbers.astype(f32))
-    )
     flops = 2 * steps * reduced * (rows + stress + 2 * modes)
     return pl.pallas_call(
         functools.partial(kernel, sectors, dofs),
         out_shape=jax.ShapeDtypeStruct((1, steps, stress), bf16),
-        in_specs=[pl.BlockSpec(memory_space=pltpu.HBM)] * 4
-        + [pl.BlockSpec(memory_space=pltpu.VMEM)],
+        in_specs=[pl.BlockSpec(memory_space=pltpu.HBM)] * 8,
         out_specs=pl.BlockSpec(memory_space=pltpu.VMEM),
         scratch_shapes=[
             pltpu.VMEM((steps, rows), bf16),
             pltpu.VMEM((HALVES, rows, half), bf16),
             pltpu.VMEM((half, modes), bf16),
             pltpu.VMEM((reduced, stress), bf16),
+            pltpu.VMEM(mode_decay.shape, f32),
+            pltpu.VMEM(mode_phase.shape, f32),
+            pltpu.SMEM((1, 1), jnp.int32),
+            pltpu.SMEM(slot_harmonic.shape, jnp.int32),
             pltpu.VMEM((steps, half), bf16),
             pltpu.VMEM((steps, half), bf16),
             pltpu.VMEM((parts, groups, ROWS, width), bf16),
@@ -388,12 +410,12 @@
             pltpu.VMEM((2, wide, wide), bf16),
             pltpu.VMEM((8, modes), f32),
             pltpu.VMEM((8, modes), f32),
-            pltpu.SemaphoreType.DMA((3 + HALVES * CHUNKS,)),
+            pltpu.SemaphoreType.DMA((7 + HALVES * CHUNKS,)),
             pltpu.SemaphoreType.DMA((7,)),
             pltpu.SemaphoreType.DMA((7,)),
         ],
         compiler_params=pltpu.CompilerParams(
-            collective_id=0, has_side_effects=True, vmem_limit_bytes=54980 * 1024
+            collective_id=0, has_side_effects=True, vmem_limit_bytes=60 * 1024 * 1024
         ),
         cost_estimate=pl.CostEstimate(
             flops=flops, bytes_accessed=2 * reduced * (rows + stress), transcendentals=0
@@ -403,7 +425,10 @@
         sector_basis,
         harmonic_modes,
         stress_basis,
-        small,
+        mode_decay,
+        mode_phase,
+        mode_count.reshape(1, 1),
+        slot_harmonic,
     )
 
 

time: 31.9 us -> 33.9 us (1.063)
  Pallas kernels: 28.9 us -> 31.2 us
  other arithmetic: 1.5 us -> 0 us
  local copies, waits for them, and re-layouts: 0.68 us -> 1.62 us
    pallas_call x1, Pallas kernels: 28.9 us -> 31.2 us  [local(): pl.pallas_call(functools.partial(kernel, sectors, dofs), out_shape=jax.Sh...]
    unnamed x1, local copies, waits for them, and re-layouts: 0.68 us -> 1.62 us
    select_n x1 -> x0, other arithmetic: 0.77 us -> none  [local(): jnp.where(row == 0, mode_decay, jnp.where(row == 1, mode_phase, numbers.a...]
    convert_element_type x1 -> x0, other arithmetic: 0.73 us -> none  [local(): numbers.astype(f32)]
where the time goes in v5:
time: 33.9 us; the launch traced here: 33.5 us
  Pallas kernels  31.2 us (92%)
  local copies, waits for them, and re-layouts  1.62 us (5%)
  between operations  0.66 us (2%)
    pallas_call x1, Pallas kernels, local(): pl.pallas_call(functools.partial(kernel, sectors, dofs), out_shape=jax.Sh...  31.2 us
    unnamed x1, local copies, waits for them, and re-layouts  1.62 us

profile of v5, /device:TPU:1, one launch (start us, length us, event | category | flops | bytes accessed | tf_op | source)
XLA Modules:
  0.0 33.5 jit_solution(4679866740508319725)
XLA Ops:
  0.7 31.2 %shard_map.82 = bf16[1,64,1536]{2,1,0:T(8,128)(2,1)} custom-call(bf16[1,64,1536]{2,1,0:T(8,128)(2,1)} %load_hbm.1, bf16[1536,1536]{1,0:T(8,128)(2,1)} %basis_hbm.1, bf16[1,1536,256]{2,1,0:T(8,128)(2,1)} %modes_hbm.1, bf16[1536,1536]{1,0:T(8,128)(2,1)} %stress_hbm.1, f32[1,256]{1,0:T(1,128)} %decay_hbm.1, f32[1,256]{1,0:T(1,128)} %phase_hbm.1, ...), custom_call_target="tpu_custom_call" | custom-call | flops 704643072 | bytes 9437184 | tf_op jit(solution)/shard_map/pallas_call | solution.py:382
  31.9 1.6 %copy.11 = bf16[1,64,1536]{2,1,0:T(8,128)(2,1)} copy(bf16[1,64,1536]{2,1,0:T(8,128)(2,1)} %shard_map.82) | data formatting | bytes 393216

commit v6 on v5

--- a/solution.py
+++ b/solution.py
@@ -25,8 +25,8 @@
             body(index)
 
 
-def farthest_first(count):
-    return sorted(range(count), key=lambda offset: -min(offset, count - offset))
+def farthest_first(index, count, own):
+    return jnp.where(own < count // 2, count - 1 - index, index)
 
 
 def kernel(
@@ -232,8 +232,8 @@
         part_send[part] = summed[:, part * width : (part + 1) * width].reshape(
             groups, ROWS, width
         )
-    for offset in farthest_first(groups):
-        group = lax.rem(own_group + offset, groups)
+    for turn in range(groups):
+        group = farthest_first(turn, groups, own_group)
         for part in range(parts):
             send_to(
                 part_send.at[part, group],
@@ -252,12 +252,11 @@
         dst = sink.at[own_group, :, pl.ds(pl.multiple_of(own_pair * width, 128), width)]
 
         def send(index):
-            swing = (index + 1) // 2
-            target = lax.rem(me + peers // 2 + (1 - index % 2 * 2) * swing, peers)
-            remote(source.at[target // parts], dst, which, device(target)).start()
-
-        each(peers - 1, send)
-        pltpu.make_async_copy(source.at[own_sector], dst, recv_sem.at[which]).start()
+            sector = farthest_first(index // parts, sectors, own_sector)
+            target = sector * parts + index % parts
+            send_to(source.at[sector], dst, which, target)
+
+        each(peers, send)
 
     @pl.when(is_mixer)
     def _():
@@ -305,8 +304,8 @@
         response, own_rows, (((1,), (1,)), ((), ())), preferred_element_type=f32
     )
     ret_send[...] = returned.astype(bf16).reshape(groups, ROWS, width)
-    for offset in farthest_first(groups):
-        group = lax.rem(own_group + offset, groups)
+    for turn in range(groups):
+        group = farthest_first(turn, groups, own_group)
         send_to(ret_send.at[group], ret_recv.at[own_sector], 4, mixer_of(group, own_pair))
 
     @pl.when(is_mixer)

time: 33.9 us -> 31.6 us (0.932)
  Pallas kernels: 31.2 us -> 29.2 us
    pallas_call x1, Pallas kernels: 31.2 us -> 29.2 us  [local(): pl.pallas_call(functools.partial(kernel, sectors, dofs), out_shape=jax.Sh...]
where the time goes in v6:
time: 31.6 us; the launch traced here: 31.5 us
  Pallas kernels  29.2 us (92%)
  local copies, waits for them, and re-layouts  1.62 us (5%)
  between operations  0.66 us (2%)
    pallas_call x1, Pallas kernels, local(): pl.pallas_call(functools.partial(kernel, sectors, dofs), out_shape=jax.Sh...  29.2 us
    unnamed x1, local copies, waits for them, and re-layouts  1.62 us

profile of v6, /device:TPU:1, one launch (start us, length us, event | category | flops | bytes accessed | tf_op | source)
XLA Modules:
  0.0 31.5 jit_solution(2080088608979105079)
XLA Ops:
  0.7 29.2 %shard_map.82 = bf16[1,64,1536]{2,1,0:T(8,128)(2,1)} custom-call(bf16[1,64,1536]{2,1,0:T(8,128)(2,1)} %load_hbm.1, bf16[1536,1536]{1,0:T(8,128)(2,1)} %basis_hbm.1, bf16[1,1536,256]{2,1,0:T(8,128)(2,1)} %modes_hbm.1, bf16[1536,1536]{1,0:T(8,128)(2,1)} %stress_hbm.1, f32[1,256]{1,0:T(1,128)} %decay_hbm.1, f32[1,256]{1,0:T(1,128)} %phase_hbm.1, ...), custom_call_target="tpu_custom_call" | custom-call | flops 704643072 | bytes 9437184 | tf_op jit(solution)/shard_map/pallas_call | solution.py:381
  29.9 1.6 %copy.11 = bf16[1,64,1536]{2,1,0:T(8,128)(2,1)} copy(bf16[1,64,1536]{2,1,0:T(8,128)(2,1)} %shard_map.82) | data formatting | bytes 393216

commit v7 on v6

--- a/solution.py
+++ b/solution.py
@@ -69,6 +69,8 @@
     local_sem,
     send_sem,
     recv_sem,
+    out_v,
+    out_sem,
 ):
     steps, reduced = load_v.shape[0], stress_v.shape[0]
     width = reduced // dofs
@@ -320,21 +322,34 @@
     back_copy = remote(back_recv, back_other, 6, sibling)
     back_copy.start()
 
-    def rows_of(which):
-        return stress_v[pl.ds(pl.multiple_of(which * half, 128), half), :]
-
-    field = jnp.dot(
-        back_recv[...].reshape(steps, half), rows_of(own_half), preferred_element_type=f32
-    )
+    piece = out_v.shape[1] // CHUNKS
+
+    def product_of(ref, which, index):
+        rows = pl.ds(pl.multiple_of(which * half, 128), half)
+        return jnp.dot(
+            ref[...].reshape(steps, half),
+            stress_v[rows, index * piece : (index + 1) * piece],
+            preferred_element_type=f32,
+        )
+
+    fields = [product_of(back_recv, own_half, index) for index in range(CHUNKS)]
     back_copy.wait_recv()
-    field = field + jnp.dot(
-        back_other[...].reshape(steps, half), rows_of(other_half), preferred_element_type=f32
-    )
-    out_ref[0] = field.astype(bf16)
+    out_copies = []
+    for index in range(CHUNKS):
+        columns = pl.ds(index * piece, piece)
+        field = fields[index] + product_of(back_other, other_half, index)
+        out_v[:, columns] = field.astype(bf16)
+        copy = pltpu.make_async_copy(
+            out_v.at[:, columns], out_ref.at[0, :, columns], out_sem.at[index]
+        )
+        copy.start()
+        out_copies.append(copy)
 
     def sent(ref, index):
         pltpu.make_async_copy(ref, ref, send_sem.at[index]).wait()
 
+    for copy in out_copies:
+        copy.wait()
     pair_copy.wait_send()
     modal_copy.wait_send()
     back_copy.wait_send()
@@ -382,7 +397,7 @@
         functools.partial(kernel, sectors, dofs),
         out_shape=jax.ShapeDtypeStruct((1, steps, stress), bf16),
         in_specs=[pl.BlockSpec(memory_space=pltpu.HBM)] * 8,
-        out_specs=pl.BlockSpec(memory_space=pltpu.VMEM),
+        out_specs=pl.BlockSpec(memory_space=pl.ANY),
         scratch_shapes=[
             pltpu.VMEM((steps, rows), bf16),
             pltpu.VMEM((HALVES, rows, half), bf16),
@@ -412,6 +427,8 @@
             pltpu.SemaphoreType.DMA((7 + HALVES * CHUNKS,)),
             pltpu.SemaphoreType.DMA((7,)),
             pltpu.SemaphoreType.DMA((7,)),
+            pltpu.VMEM((steps, stress), bf16),
+            pltpu.SemaphoreType.DMA((CHUNKS,)),
         ],
         compiler_params=pltpu.CompilerParams(
             collective_id=0, has_side_effects=True, vmem_limit_bytes=60 * 1024 * 1024

time: 31.6 us -> 31.6 us (level)
  no operation moved by 1% of the time
where the time goes in v7:
time: 31.6 us; the launch traced here: 31.5 us
  Pallas kernels  29.2 us (92%)
  local copies, waits for them, and re-layouts  1.62 us (5%)
  between operations  0.66 us (2%)
    pallas_call x1, Pallas kernels, local(): pl.pallas_call(functools.partial(kernel, sectors, dofs), out_shape=jax.Sh...  29.2 us
    unnamed x1, local copies, waits for them, and re-layouts  1.62 us

profile of v7, /device:TPU:1, one launch (start us, length us, event | category | flops | bytes accessed | tf_op | source)
XLA Modules:
  0.0 31.5 jit_solution(2950217757397470459)
XLA Ops:
  0.7 29.2 %shard_map.82 = bf16[1,64,1536]{2,1,0:T(8,128)(2,1)} custom-call(bf16[1,64,1536]{2,1,0:T(8,128)(2,1)} %load_hbm.1, bf16[1536,1536]{1,0:T(8,128)(2,1)} %basis_hbm.1, bf16[1,1536,256]{2,1,0:T(8,128)(2,1)} %modes_hbm.1, bf16[1536,1536]{1,0:T(8,128)(2,1)} %stress_hbm.1, f32[1,256]{1,0:T(1,128)} %decay_hbm.1, f32[1,256]{1,0:T(1,128)} %phase_hbm.1, ...), custom_call_target="tpu_custom_call" | custom-call | flops 704643072 | bytes 9437184 | tf_op jit(solution)/shard_map/pallas_call | solution.py:396
  29.9 1.6 %copy.11 = bf16[1,64,1536]{2,1,0:T(8,128)(2,1)} copy(bf16[1,64,1536]{2,1,0:T(8,128)(2,1)} %shard_map.82) | data formatting | bytes 393216

commit v8 on v7

--- a/solution.py
+++ b/solution.py
@@ -225,18 +225,18 @@
 
     pair_copy = remote(pair_send, pair_recv, 0, sibling)
     pair_copy.start()
-    product = partial_product(1)
+    for copy in basis_copies[1]:
+        copy.wait()
+    product = jnp.dot(load_v[...], basis_v[1], preferred_element_type=f32)
     modes_copy = load(modes_hbm.at[0, columns_of(own_half), :], modes_v, 5)
     stress_copy = load(stress_hbm, stress_v, 6)
     pair_copy.wait_recv()
-    summed = (product + pair_recv[...].astype(f32)).astype(bf16)
     for part in range(parts):
-        part_send[part] = summed[:, part * width : (part + 1) * width].reshape(
-            groups, ROWS, width
-        )
-    for turn in range(groups):
-        group = farthest_first(turn, groups, own_group)
-        for part in range(parts):
+        columns = slice(part * width, (part + 1) * width)
+        summed = (product[:, columns] + pair_recv[:, columns].astype(f32)).astype(bf16)
+        part_send[part] = summed.reshape(groups, ROWS, width)
+        for turn in range(groups):
+            group = farthest_first(turn, groups, own_group)
             send_to(
                 part_send.at[part, group],
                 part_recv.at[own_sector, own_pair],

time: 31.6 us -> 31.4 us (level)
  no operation moved by 1% of the time
where the time goes in v8:
time: 31.4 us; the launch traced here: 31.2 us
  Pallas kernels  29 us (92%)
  local copies, waits for them, and re-layouts  1.62 us (5%)
  between operations  0.66 us (2%)
    pallas_call x1, Pallas kernels, local(): pl.pallas_call(functools.partial(kernel, sectors, dofs), out_shape=jax.Sh...  29 us
    unnamed x1, local copies, waits for them, and re-layouts  1.62 us

profile of v8, /device:TPU:1, one launch (start us, length us, event | category | flops | bytes accessed | tf_op | source)
XLA Modules:
  0.0 31.2 jit_solution(17040238007049590374)
XLA Ops:
  0.7 29.0 %shard_map.82 = bf16[1,64,1536]{2,1,0:T(8,128)(2,1)} custom-call(bf16[1,64,1536]{2,1,0:T(8,128)(2,1)} %load_hbm.1, bf16[1536,1536]{1,0:T(8,128)(2,1)} %basis_hbm.1, bf16[1,1536,256]{2,1,0:T(8,128)(2,1)} %modes_hbm.1, bf16[1536,1536]{1,0:T(8,128)(2,1)} %stress_hbm.1, f32[1,256]{1,0:T(1,128)} %decay_hbm.1, f32[1,256]{1,0:T(1,128)} %phase_hbm.1, ...), custom_call_target="tpu_custom_call" | custom-call | flops 704643072 | bytes 9437184 | tf_op jit(solution)/shard_map/pallas_call | solution.py:396
  29.6 1.6 %copy.11 = bf16[1,64,1536]{2,1,0:T(8,128)(2,1)} copy(bf16[1,64,1536]{2,1,0:T(8,128)(2,1)} %shard_map.82) | data formatting | bytes 393216
